TPU v7x, 256 devices: a whole 4x4x8 slice. The times are simulated.
256 devices in a mesh: gx: 32 (over x_hi, z, core), gy: 8 (over y, x_lo).
Axes of the slice: x: 4 (x_hi: 2, x_lo: 2; x = x_hi * 2 + x_lo), y: 4, z: 8, core: 2. Of those that a mesh axis runs over, the one named last changes fastest.
Arguments:
- fields: float32 [64, 2304, 2000], P(None, 'gx', 'gy'), may hold values from -6 to 6
Outputs:
- spectrum: float32 [2, 64, 1152, 2000], P(None, 'gx', 'gy')
All inputs are finite; a program needn't handle non-finite values.
Results may differ from a plain program's by a relative error of at most 0.00007.
Values sent between devices are 32-bit elements; how exact they have to be, the bound alone decides.
No kernel may reach another device: no remote copies, remote signals or barrier semaphores. Data moves between devices by JAX's collectives and lax.ppermute only.
A program may use at most 128 MiB of HBM per device.

v0:
```python
import functools
import math

import jax
import jax.numpy as jnp
import ml_dtypes
import numpy as np
from jax import lax
from jax.experimental import pallas as pl
from jax.experimental.pallas import tpu as pltpu
from jax.sharding import PartitionSpec as P

NX = 2304
NY = 2000
KX = 1152
HALF = NX // 2
STRIP = 72
LANES = 128
ROWS = 250
NJ = 8
NZ = 8
VMEM = 48 * 1024 * 1024


def split_table(table):
    high = table.astype(np.float32).astype(ml_dtypes.bfloat16)
    low = (table - high.astype(np.float64)).astype(np.float32).astype(ml_dtypes.bfloat16)
    return high, low


@functools.cache
def x_table():
    b = np.arange(HALF)
    steps = []
    for p in range(2):
        for m in range(2):
            block = np.arange(4)[:, None] + 4 * m
            k = (144 * block + 2 * np.arange(STRIP)[None, :] + p).reshape(-1)
            angle = 2.0 * np.pi / NX * ((k[:, None] * b[None, :]) % NX)
            both = np.stack([np.cos(angle).reshape(4, STRIP, HALF), -np.sin(angle).reshape(4, STRIP, HALF)], axis=1)
            high, low = split_table(both.reshape(-1, HALF) / math.sqrt(NX))
            steps.append(np.concatenate([high, low], axis=0))
    return np.stack(steps)


@functools.cache
def y_tables():
    b = np.arange(2 * LANES)
    twist = 2.0 * np.pi / NY * ((np.arange(NJ)[:, None] * b[None, :]) % NY)
    twiddle = np.stack([np.cos(twist), np.sin(twist)], axis=1)
    twiddle = twiddle.reshape(NJ, 2, 2, LANES).transpose(2, 0, 1, 3).astype(np.float32)
    d = np.arange(2 * LANES)
    angle = 2.0 * np.pi / ROWS * ((b[:, None] * d[None, :]) % ROWS)
    keep = ((b < ROWS)[:, None] & (d < ROWS)[None, :]).astype(np.float64) / math.sqrt(NY)
    cosine, sine = np.cos(angle) * keep, np.sin(angle) * keep
    from_real = np.concatenate([cosine, -sine], axis=1)
    from_imag = np.concatenate([sine, cosine], axis=1)
    rows = np.concatenate([from_real[:LANES], from_imag[:LANES], from_real[LANES:], from_imag[LANES:]], axis=0)
    main = np.stack(split_table(rows))
    weave = np.zeros((4, 2 * LANES, 2 * LANES), np.float32)
    for t in range(4):
        for upper in range(2):
            for lane in range(LANES):
                c = 4 * upper + (lane // 32 - t) % 4
                weave[t, upper * LANES + lane, 8 * (lane % 32) + c] = 1.0
    return twiddle, main, weave.astype(ml_dtypes.bfloat16)


def compiler_params():
    return pltpu.CompilerParams(vmem_limit_bytes=VMEM)


def store_lanes(out, value, half):
    if half == 0:
        out[...] = value
    else:
        out[...] = jnp.zeros(out.shape, out.dtype)
        out[..., : ROWS - LANES] = value


def pack_first(fields):
    def kernel(a, out):
        for hi in range(2):
            for core in range(2):
                out[hi, :, core] = a[hi, :, 2 * core]

    return pl.pallas_call(
        kernel,
        grid=(4,),
        out_shape=jax.ShapeDtypeStruct((2, NZ, 2, STRIP, LANES), jnp.float32),
        in_specs=[pl.BlockSpec((2, 2, 4, STRIP, LANES), lambda i: (0, i, 0, 0, 0))],
        out_specs=pl.BlockSpec((2, 2, 2, STRIP, LANES), lambda i: (0, i, 0, 0, 0)),
        compiler_params=compiler_params(),
        name="pack_first",
    )(fields)


CHUNKS = ((0, 1), (1, 0), (1, 1))
PARTNERS = ((0, 0), (0, 1), (1, 0), (1, 1))


def pack_rest(place, fields):
    def kernel(place, a, *outs):
        hi, core = place[0], place[2]
        index = 0
        for field, half in CHUNKS:
            for dh, dc in PARTNERS:
                to_hi = lax.rem(hi + dh, 2)
                to_core = lax.rem(core + dc, 2)
                lanes = slice(0, LANES) if half == 0 else slice(LANES, ROWS)
                store_lanes(outs[index], a[pl.ds(to_hi, 1), 0, pl.ds(2 * to_core + field, 1), :, lanes][0], half)
                index += 1

    shape = jax.ShapeDtypeStruct((NZ, STRIP, LANES), jnp.float32)
    spec = pl.BlockSpec((1, STRIP, LANES), lambda i, place: (i, 0, 0))
    return pl.pallas_call(
        kernel,
        grid_spec=pltpu.PrefetchScalarGridSpec(
            num_scalar_prefetch=1,
            grid=(NZ,),
            in_specs=[pl.BlockSpec((2, 1, 4, STRIP, ROWS), lambda i, place: (0, i, 0, 0, 0))],
            out_specs=[spec] * 12,
        ),
        out_shape=[shape] * 12,
        compiler_params=compiler_params(),
        name="pack_rest",
    )(place, fields)


def pack_z(place, parts):
    def kernel(place, *refs):
        sources, outs, sem = refs[:4], refs[4:11], refs[11]
        copies = []
        for dz in range(1, NZ):
            to_z = lax.rem(place[1] + dz, NZ)
            for i in range(4):
                copies.append(pltpu.make_async_copy(sources[i].at[to_z], outs[dz - 1].at[i], sem))
        for copy in copies:
            copy.start()
        for copy in copies:
            copy.wait()

    shape = jax.ShapeDtypeStruct((4, STRIP, LANES), jnp.float32)
    anywhere = pl.BlockSpec(memory_space=pl.ANY)
    return pl.pallas_call(
        kernel,
        in_specs=[pl.BlockSpec(memory_space=pltpu.SMEM)] + [anywhere] * 4,
        out_specs=[anywhere] * 7,
        out_shape=[shape] * 7,
        scratch_shapes=[pltpu.SemaphoreType.DMA],
        compiler_params=compiler_params(),
        name="pack_z",
    )(place, *parts)


def x_transform(place, pieces):
    whole = len(pieces) == 1

    def kernel(place, *refs):
        sources = refs[: len(pieces)]
        table, out, columns, folded, sem = refs[len(pieces) :]
        step = pl.program_id(0)

        @pl.when(step == 0)
        def _():
            copies = []
            if whole:
                copies.append(pltpu.make_async_copy(sources[0], columns, sem))
            else:
                hi, z, core = place[0], place[1], place[2]
                for i, (dh, dc) in enumerate(PARTNERS):
                    from_hi = lax.rem(hi + dh, 2)
                    from_core = lax.rem(core + dc, 2)
                    for dz in range(NZ):
                        from_z = lax.rem(z + NZ - dz, NZ)
                        source = sources[i].at[z] if dz == 0 else sources[3 + dz].at[i]
                        start = pl.multiple_of(STRIP * (from_hi * 16 + from_z * 2 + from_core), 8)
                        copies.append(pltpu.make_async_copy(source, columns.at[pl.ds(start, STRIP)], sem))
            for copy in copies:
                copy.start()
            for copy in copies:
                copy.wait()
            first = columns[:HALF]
            second = columns[HALF:]
            for p, value in enumerate((first + second, first - second)):
                high = value.astype(jnp.bfloat16)
                low = (value - high.astype(jnp.float32)).astype(jnp.bfloat16)
                folded[p, :, :LANES] = high
                folded[p, :, LANES:] = low

        product = jnp.dot(table[0], folded[step // 2], preferred_element_type=jnp.float32)
        upper = product[: HALF // 2]
        lower = product[HALF // 2 :]
        total = upper[:, :LANES] + (upper[:, LANES:] + lower[:, :LANES])
        out[...] = total.reshape(4, 2, 1, STRIP, LANES)

    anywhere = pl.BlockSpec(memory_space=pl.ANY)
    return pl.pallas_call(
        kernel,
        grid_spec=pltpu.PrefetchScalarGridSpec(
            num_scalar_prefetch=1,
            grid=(4,),
            in_specs=[anywhere] * len(pieces) + [pl.BlockSpec((1, HALF, HALF), lambda s, place: (s, 0, 0))],
            out_specs=pl.BlockSpec((4, 2, 1, STRIP, LANES), lambda s, place: (s % 2, 0, s // 2, 0, 0)),
            scratch_shapes=[
                pltpu.VMEM((NX, LANES), jnp.float32),
                pltpu.VMEM((2, HALF, 2 * LANES), jnp.bfloat16),
                pltpu.SemaphoreType.DMA,
            ],
        ),
        out_shape=jax.ShapeDtypeStruct((NJ, 2, 2, STRIP, LANES), jnp.float32),
        compiler_params=compiler_params(),
        name="x_transform",
    )(place, *pieces, jnp.asarray(x_table()))


def eight_point(re, im):
    def add(a, b):
        return a[0] + b[0], a[1] + b[1]

    def sub(a, b):
        return a[0] - b[0], a[1] - b[1]

    def four(v):
        s, d = add(v[0], v[2]), sub(v[0], v[2])
        t, e = add(v[1], v[3]), sub(v[1], v[3])
        turned = e[1], -e[0]
        return add(s, t), add(d, turned), sub(s, t), sub(d, turned)

    values = list(zip(re, im))
    even = four(values[0::2])
    odd = four(values[1::2])
    root = math.sqrt(0.5)
    o1 = (odd[1][0] + odd[1][1]) * root, (odd[1][1] - odd[1][0]) * root
    o2 = odd[2][1], -odd[2][0]
    o3 = (odd[3][1] - odd[3][0]) * root, (odd[3][0] + odd[3][1]) * -root
    odd = odd[0], o1, o2, o3
    return [add(e, o) for e, o in zip(even, odd)] + [sub(e, o) for e, o in zip(even, odd)]


TILE = 16


def y_kernel(first, second, twiddle, main, weave, *refs):
    out, high, low, mixed, woven = refs[-5:]
    for half, source in enumerate((first, second)):

        def fold(i, carry, half=half, source=source):
            rows = pl.ds(pl.multiple_of(i * TILE, TILE), TILE)
            re = [source[j, 0, rows, :] for j in range(NJ)]
            im = [source[j, 1, rows, :] for j in range(NJ)]
            for c, (a, b) in enumerate(eight_point(re, im)):
                if c > 0:
                    cosine = twiddle[half, c, 0:1, :]
                    sine = twiddle[half, c, 1:2, :]
                    a, b = a * cosine + b * sine, b * cosine - a * sine
                for comp, value in enumerate((a, b)):
                    lanes = slice((2 * half + comp) * LANES, (2 * half + comp + 1) * LANES)
                    top = value.astype(jnp.bfloat16)
                    high[c, rows, lanes] = top
                    low[c, rows, lanes] = (value - top.astype(jnp.float32)).astype(jnp.bfloat16)
            return carry

        lax.fori_loop(0, 144 // TILE, fold, 0)

    for c in range(NJ):
        a = high[c]
        value = (
            jnp.dot(a, main[0], preferred_element_type=jnp.float32)
            + jnp.dot(low[c], main[0], preferred_element_type=jnp.float32)
            + jnp.dot(a, main[1], preferred_element_type=jnp.float32)
        )
        for part in range(4):
            piece = value[:, part * LANES : (part + 1) * LANES]
            if c % 4 > 0:
                piece = pltpu.roll(piece, 32 * (c % 4), 1)
            for p in range(2):
                mixed[c, part, pl.ds(p, STRIP, stride=2), :] = piece[p * STRIP : (p + 1) * STRIP]

    slot = lax.broadcasted_iota(jnp.int32, (144, LANES), 1) // 32
    for t in range(4):
        for comp in range(2):
            for upper in range(2):
                part = 2 * comp + upper
                for group in range(2):
                    value = mixed[4 * group, part]
                    for c in range(1, 4):
                        value = jnp.where(slot == (c + t) % 4, mixed[4 * group + c, part], value)
                    top = value.astype(jnp.bfloat16)
                    start = part * 144
                    columns = slice(group * LANES, (group + 1) * LANES)
                    woven[start : start + 144, columns] = top
                    woven[start + 576 : start + 720, columns] = (value - top.astype(jnp.float32)).astype(jnp.bfloat16)
        product = jnp.dot(woven[...], weave[t], preferred_element_type=jnp.float32)
        product = product[:576] + product[576:]
        for comp in range(2):
            for upper in range(2):
                tile = 4 * upper + t
                width = min(256, NY - 256 * tile)
                start = (2 * comp + upper) * 144
                out[comp, 0, :, 256 * tile : 256 * tile + width] = product[start : start + 144, :width]


def y_transform(field, halves, before):
    twiddle, main, weave = y_tables()
    whole = pl.BlockSpec(memory_space=pltpu.VMEM)
    inputs = [*halves, jnp.asarray(twiddle), jnp.asarray(main), jnp.asarray(weave)]
    block = pl.BlockSpec((2, 1, 144, NY), lambda i: (0, field, 0, 0))

    def full(array):
        zeros = (0,) * array.ndim
        return pl.BlockSpec(array.shape, lambda i: zeros)

    in_specs = [full(array) for array in inputs]
    aliases = {}
    if before is not None:
        aliases = {len(inputs): 0}
        inputs.append(before)
        in_specs.append(pl.BlockSpec(memory_space=pl.ANY))
    return pl.pallas_call(
        y_kernel,
        grid=(1,),
        in_specs=in_specs,
        out_specs=block,
        out_shape=jax.ShapeDtypeStruct((2, 2, 144, NY), jnp.float32),
        scratch_shapes=[
            pltpu.VMEM((NJ, 144, 512), jnp.bfloat16),
            pltpu.VMEM((NJ, 144, 512), jnp.bfloat16),
            pltpu.VMEM((NJ, 4, 144, LANES), jnp.float32),
            pltpu.VMEM((1152, 256), jnp.bfloat16),
        ],
        input_output_aliases=aliases,
        compiler_params=compiler_params(),
        name="y_transform",
    )(*inputs)


def shift(dh, dz, dc):
    pairs = []
    for hi in range(2):
        for z in range(NZ):
            for core in range(2):
                to = (hi + dh) % 2 * 16 + (z + dz) % NZ * 2 + (core + dc) % 2
                pairs.append((hi * 16 + z * 2 + core, to))
    return pairs


def over_y(blocks):
    blocks = blocks.reshape(NJ, 2, 144, LANES)
    return lax.all_to_all(blocks, "gy", split_axis=0, concat_axis=0, tiled=True)


Z_ORDER = (4, 3, 5, 2, 6, 1, 7)


def body(fields):
    me = lax.axis_index("gx")
    place = jnp.stack([me // 16, me // 2 % NZ, me % 2]).astype(jnp.int32)
    fields = fields.reshape(2, NZ, 4, STRIP, ROWS)
    first = pack_first(fields).reshape(32, STRIP, LANES)
    first = lax.all_to_all(first, "gx", split_axis=0, concat_axis=0, tiled=True)
    packed = pack_rest(place, fields)
    spectra = [over_y(x_transform(place, [first.reshape(NX, LANES)]))]
    for chunk in range(3):
        own, *away = packed[4 * chunk : 4 * chunk + 4]
        parts = [own]
        for (dh, dc), part in zip(PARTNERS[1:], away):
            parts.append(lax.ppermute(part, "gx", shift(dh, 0, dc)))
        sends = pack_z(place, parts)
        received = [None] * 7
        for dz in Z_ORDER:
            received[dz - 1] = lax.ppermute(sends[dz - 1], "gx", shift(0, dz, 0))
        spectra.append(over_y(x_transform(place, parts + received)))
    result = y_transform(0, spectra[:2], None)
    return y_transform(1, spectra[2:], result)


def solution(mesh):
    in_specs = (P(None, "gx", "gy"),)
    out_specs = P(None, "gx", "gy", None)
    return jax.shard_map(body, mesh=mesh, in_specs=in_specs, out_specs=out_specs, check_vma=False)
```

profile of v0, /device:TPU:68, one launch (start us, length us, event | category | flops | bytes accessed | tf_op | source)
XLA Modules:
  0.0 309.6 jit_solution(16565249563030950325)
XLA Ops:
  0.1 5.4 %pack_rest.1 = (f32[8,72,128]{2,1,0:T(8,128)S(1)}, f32[8,72,128]{2,1,0:T(8,128)S(1)}, f32[8,72,128]{2,1,0:T(8,128)S(1)}, f32[8,72,128]{2,1,0:T(8,128)S(1)}, f32[...) custom-call(s32[3]{0:T(128)S(1)} %pad_add_fusion.place, ...), custom_call_target="tpu_custom_call" | custom-call | tf_op jit(solution)/shard_map/pack_rest/pallas_call | solution.py:116
  10.3 8.0 %collective-permute-done.21.refs_2_ = f32[8,72,128]{2,1,0:T(8,128)S(1)} collective-permute-done((f32[8,72,128]{2,1,0:T(8,128)S(1)}, f32[8,72,128]{2,1,0:T(8,128)S(1)}, u32[]{:S(2)}, u32[]{:S(2)}) %collective-permute-start.21) | collective-permute-done | bytes 294944 | tf_op jit(solution)/shard_map/ppermute | solution.py:368
  18.3 5.4 %collective-permute-done.22.refs_3_ = f32[8,72,128]{2,1,0:T(8,128)S(1)} collective-permute-done((f32[8,72,128]{2,1,0:T(8,128)S(1)}, f32[8,72,128]{2,1,0:T(8,128)S(1)}, u32[]{:S(2)}, u32[]{:S(2)}) %collective-permute-start.22) | collective-permute-done | bytes 294944 | tf_op jit(solution)/shard_map/ppermute | solution.py:368
  42.6 8.7 %collective-permute-done.25.refs_6_ = f32[4,72,128]{2,1,0:T(8,128)S(1)} collective-permute-done((f32[4,72,128]{2,1,0:T(8,128)S(1)}, f32[4,72,128]{2,1,0:T(8,128)S(1)}, u32[]{:S(2)}, u32[]{:S(2)}) %collective-permute-start.25) | collective-permute-done | bytes 147488 | tf_op jit(solution)/shard_map/ppermute | solution.py:372
  51.3 7.0 %collective-permute-done.26.refs_7_ = f32[4,72,128]{2,1,0:T(8,128)S(1)} collective-permute-done((f32[4,72,128]{2,1,0:T(8,128)S(1)}, f32[4,72,128]{2,1,0:T(8,128)S(1)}, u32[]{:S(2)}, u32[]{:S(2)}) %collective-permute-start.26) | collective-permute-done | bytes 147488 | tf_op jit(solution)/shard_map/ppermute | solution.py:372
  63.0 10.1 %x_transform.7 = f32[8,2,2,72,128]{4,3,2,1,0:T(8,128)} custom-call(s32[3]{0:T(128)S(1)} %pad_add_fusion.place, f32[8,72,128]{2,1,0:T(8,128)S(1)} %get-tuple-element.60.refs_0_, f32[8,72,128]{2,1,0:T(8,128)S(1)} %collective-permute-done.20.refs_1_, f32[8,72,128]{2,1,0:T(8,128)S(1)} %collective-permute-done.21.refs_2_, ...), custom_call_target="tpu_custom_call" | custom-call | tf_op jit(solution)/shard_map/x_transform/pallas_call | solution.py:198
  73.1 5.1 %all-to-all-start.4 = ((f32[8,2,144,128]{3,2,1,0:T(8,128)}), f32[8,2,144,128]{3,2,1,0:T(8,128)S(1)}, u32[]{:S(2)}, u32[]{:S(2)}) async-start(f32[8,2,144,128]{3,2,1,0:T(8,128)} %bitcast.9), calls=%async_computation.4 | async-start | bytes 2359296 | tf_op jit(solution)/shard_map/all_to_all | solution.py:350
  82.3 12.2 %all-to-all-done.4.second = f32[8,2,144,128]{3,2,1,0:T(8,128)S(1)} async-done(((f32[8,2,144,128]{3,2,1,0:T(8,128)}), f32[8,2,144,128]{3,2,1,0:T(8,128)S(1)}, u32[]{:S(2)}, u32[]{:S(2)}) %all-to-all-start.4) | async-done | bytes 1179680 | tf_op jit(solution)/shard_map/all_to_all | solution.py:350
  94.5 8.4 %all-to-all-start.2 = ((f32[32,72,128]{2,1,0:T(8,128)}), f32[32,72,128]{2,1,0:T(8,128)S(1)}, u32[]{:S(2)}, u32[]{:S(2)}) async-start(f32[32,72,128]{2,1,0:T(8,128)} %bitcast.6), calls=%async_computation.2 | async-start | bytes 2359296 | tf_op jit(solution)/shard_map/all_to_all | solution.py:361
  106.4 13.8 %collective-permute-done.11.refs_2_ = f32[8,72,128]{2,1,0:T(8,128)S(1)} collective-permute-done((f32[8,72,128]{2,1,0:T(8,128)S(1)}, f32[8,72,128]{2,1,0:T(8,128)S(1)}, u32[]{:S(2)}, u32[]{:S(2)}) %collective-permute-start.11) | collective-permute-done | bytes 294944 | tf_op jit(solution)/shard_map/ppermute | solution.py:368
  120.2 9.4 %collective-permute-done.12.refs_3_ = f32[8,72,128]{2,1,0:T(8,128)S(1)} collective-permute-done((f32[8,72,128]{2,1,0:T(8,128)S(1)}, f32[8,72,128]{2,1,0:T(8,128)S(1)}, u32[]{:S(2)}, u32[]{:S(2)}) %collective-permute-start.12) | collective-permute-done | bytes 294944 | tf_op jit(solution)/shard_map/ppermute | solution.py:368
  136.6 5.1 %collective-permute-start.16 = (f32[4,72,128]{2,1,0:T(8,128)S(1)}, f32[4,72,128]{2,1,0:T(8,128)S(1)}, u32[]{:S(2)}, u32[]{:S(2)}) collective-permute-start(f32[4,72,128]{2,1,0:T(8,128)S(1)} %get-tuple-element.56), channel_id=1, source_target_pairs={{0,64},{8,72},{16,80},{24,88},{32,96},{40,104},{48,112},{56,120},{... | collective-permute-start | bytes 442376 | tf_op jit(solution)/shard_map/ppermute | solution.py:372
  145.9 10.2 %collective-permute-done.15.refs_6_ = f32[4,72,128]{2,1,0:T(8,128)S(1)} collective-permute-done((f32[4,72,128]{2,1,0:T(8,128)S(1)}, f32[4,72,128]{2,1,0:T(8,128)S(1)}, u32[]{:S(2)}, u32[]{:S(2)}) %collective-permute-start.15) | collective-permute-done | bytes 147488 | tf_op jit(solution)/shard_map/ppermute | solution.py:372
  156.0 5.8 %collective-permute-done.16.refs_7_ = f32[4,72,128]{2,1,0:T(8,128)S(1)} collective-permute-done((f32[4,72,128]{2,1,0:T(8,128)S(1)}, f32[4,72,128]{2,1,0:T(8,128)S(1)}, u32[]{:S(2)}, u32[]{:S(2)}) %collective-permute-start.16) | collective-permute-done | bytes 147488 | tf_op jit(solution)/shard_map/ppermute | solution.py:372
  169.4 9.3 %x_transform.5 = f32[8,2,2,72,128]{4,3,2,1,0:T(8,128)S(1)} custom-call(s32[3]{0:T(128)S(1)} %pad_add_fusion.place, f32[8,72,128]{2,1,0:T(8,128)S(1)} %copy-done.13, f32[8,72,128]{2,1,0:T(8,128)S(1)} %collective-permute-done.10.refs_1_, f32[8,72,128]{2,1,0:T(8,128)S(1)} %collective-permute-done.11.refs_2_, f32[8,72,128]{2,1,0:T(8,128)S(1)} %collective-permute-done.12.refs_3_, ...), custom_call_target="tpu_custom_call" | custom-call | tf_op jit(solution)/shard_map/x_transform/pallas_call | solution.py:198
  183.4 8.5 %x_transform.6 = f32[8,2,2,72,128]{4,3,2,1,0:T(8,128)} custom-call(s32[3]{0:T(128)S(1)} %pad_add_fusion.place, f32[2304,128]{1,0:T(8,128)S(1)} %bitcast.12, bf16[4,1152,1152]{2,1,0:T(8,128)(2,1)} %constant.59.clone.refs_11_.refs_1_), custom_call_target="tpu_custom_call" | custom-call | tf_op jit(solution)/shard_map/x_transform/pallas_call | solution.py:198
  191.9 7.7 %all-to-all-done.1.second = f32[8,2,144,128]{3,2,1,0:T(8,128)S(1)} async-done(((f32[8,2,144,128]{3,2,1,0:T(8,128)}), f32[8,2,144,128]{3,2,1,0:T(8,128)S(1)}, u32[]{:S(2)}, u32[]{:S(2)}) %all-to-all-start.1) | async-done | bytes 1179680 | tf_op jit(solution)/shard_map/all_to_all | solution.py:350
  206.6 19.5 %collective-permute-done.1.refs_2_ = f32[8,72,128]{2,1,0:T(8,128)S(1)} collective-permute-done((f32[8,72,128]{2,1,0:T(8,128)}, f32[8,72,128]{2,1,0:T(8,128)S(1)}, u32[]{:S(2)}, u32[]{:S(2)}) %collective-permute-start.1) | collective-permute-done | bytes 294944 | tf_op jit(solution)/shard_map/ppermute | solution.py:368
  250.1 13.1 %collective-permute-done.6.refs_7_ = f32[4,72,128]{2,1,0:T(8,128)S(1)} collective-permute-done((f32[4,72,128]{2,1,0:T(8,128)S(1)}, f32[4,72,128]{2,1,0:T(8,128)S(1)}, u32[]{:S(2)}, u32[]{:S(2)}) %collective-permute-start.6) | collective-permute-done | bytes 147488 | tf_op jit(solution)/shard_map/ppermute | solution.py:372
  267.2 9.3 %x_transform.4 = f32[8,2,2,72,128]{4,3,2,1,0:T(8,128)S(1)} custom-call(s32[3]{0:T(128)S(1)} %pad_add_fusion.place, f32[8,72,128]{2,1,0:T(8,128)S(1)} %copy-done.11, f32[8,72,128]{2,1,0:T(8,128)S(1)} %collective-permute-done.refs_1_, f32[8,72,128]{2,1,0:T(8,128)S(1)} %collective-permute-done.1.refs_2_, f32[8,72,128]{2,1,0:T(8,128)S(1)} %collective-permute-done.2.refs_3_, ...), custom_call_target="tpu_custom_call" | custom-call | tf_op jit(solution)/shard_map/x_transform/pallas_call | solution.py:198
  278.6 5.8 %all-to-all-start = ((f32[8,2,144,128]{3,2,1,0:T(8,128)}), f32[8,2,144,128]{3,2,1,0:T(8,128)S(1)}, u32[]{:S(2)}, u32[]{:S(2)}) async-start(f32[8,2,144,128]{3,2,1,0:T(8,128)} %bitcast.13), calls=%async_computation | async-start | bytes 2359296 | tf_op jit(solution)/shard_map/all_to_all | solution.py:350
  287.9 5.6 %y_transform.2.refs_0_ = f32[2,2,144,2000]{3,2,1,0:T(8,128)} custom-call(f32[8,2,144,128]{3,2,1,0:T(8,128)S(1)} %copy-done.2, f32[8,2,144,128]{3,2,1,0:T(8,128)S(1)} %all-to-all-done.4.second, f32[2,8,2,128]{3,2,1,0:T(2,128)S(1)} %copy-done.14, bf16[2,512,512]{2,1,0:T(8,128)(2,1)S(1)} %copy-done.5, bf16[4,256,256]{2,1,0:T(8,128)(2,1)S(1)} %copy-done.7), custom_call_target="tpu_custom_call" | custom-call | tf_op jit(solution)/shard_map/y_transform/pallas_call | solution.py:320
  293.4 8.3 %all-to-all-done.first = f32[8,2,144,128]{3,2,1,0:T(8,128)S(1)} async-done(((f32[8,2,144,128]{3,2,1,0:T(8,128)}), f32[8,2,144,128]{3,2,1,0:T(8,128)S(1)}, u32[]{:S(2)}, u32[]{:S(2)}) %all-to-all-start) | async-done | bytes 1179680 | tf_op jit(solution)/shard_map/all_to_all | solution.py:350
  304.0 5.6 %y_transform.3 = f32[2,2,144,2000]{3,2,1,0:T(8,128)} custom-call(f32[8,2,144,128]{3,2,1,0:T(8,128)S(1)} %all-to-all-done.first, f32[8,2,144,128]{3,2,1,0:T(8,128)S(1)} %all-to-all-done.1.second, f32[2,8,2,128]{3,2,1,0:T(2,128)S(1)} %copy-done.14, bf16[2,512,512]{2,1,0:T(8,128)(2,1)S(1)} %copy-done.6, ...), custom_call_target="tpu_custom_call", output_to_operand_aliasing={{}: (5, {})} | custom-call | tf_op jit(solution)/shard_map/y_transform/pallas_call | solution.py:320
  (94 shorter events, 102.2 us)
Async XLA Ops:
  31.2 20.1 %collective-permute-start.25 = (f32[4,72,128]{2,1,0:T(8,128)S(1)}, f32[4,72,128]{2,1,0:T(8,128)S(1)}, u32[]{:S(2)}, u32[]{:S(2)}) collective-permute-start(f32[4,72,128]{2,1,0:T(8,128)S(1)} %get-tuple-element.66), channel_id=1, source_target_pairs={{0,48},{8,56},{16,64},{24,72},{32,80},{40,88},{48,96},{56,104},{64... | collective-permute-start | bytes 442376 | tf_op jit(solution)/shard_map/ppermute | solution.py:372
  32.2 26.1 %collective-permute-start.26 = (f32[4,72,128]{2,1,0:T(8,128)S(1)}, f32[4,72,128]{2,1,0:T(8,128)S(1)}, u32[]{:S(2)}, u32[]{:S(2)}) collective-permute-start(f32[4,72,128]{2,1,0:T(8,128)S(1)} %get-tuple-element.67), channel_id=1, source_target_pairs={{0,64},{8,72},{16,80},{24,88},{32,96},{40,104},{48,112},{56,120},{... | collective-permute-start | bytes 442376 | tf_op jit(solution)/shard_map/ppermute | solution.py:372
  36.7 21.6 %collective-permute-start.27 = (f32[4,72,128]{2,1,0:T(8,128)S(1)}, f32[4,72,128]{2,1,0:T(8,128)S(1)}, u32[]{:S(2)}, u32[]{:S(2)}) collective-permute-start(f32[4,72,128]{2,1,0:T(8,128)S(1)} %get-tuple-element.68), channel_id=1, source_target_pairs={{0,80},{8,88},{16,96},{24,104},{32,112},{40,120},{48,0},{56,8},{64... | collective-permute-start | bytes 442376 | tf_op jit(solution)/shard_map/ppermute | solution.py:372
  37.2 23.1 %collective-permute-start.28 = (f32[4,72,128]{2,1,0:T(8,128)S(1)}, f32[4,72,128]{2,1,0:T(8,128)S(1)}, u32[]{:S(2)}, u32[]{:S(2)}) collective-permute-start(f32[4,72,128]{2,1,0:T(8,128)S(1)} %get-tuple-element.69), channel_id=1, source_target_pairs={{0,96},{8,104},{16,112},{24,120},{32,0},{40,8},{48,16},{56,24},{64... | collective-permute-start | bytes 442376 | tf_op jit(solution)/shard_map/ppermute | solution.py:372
  42.4 20.6 %collective-permute-start.29 = (f32[4,72,128]{2,1,0:T(8,128)S(1)}, f32[4,72,128]{2,1,0:T(8,128)S(1)}, u32[]{:S(2)}, u32[]{:S(2)}) collective-permute-start(f32[4,72,128]{2,1,0:T(8,128)S(1)} %get-tuple-element.70), channel_id=1, source_target_pairs={{0,112},{8,120},{16,0},{24,8},{32,16},{40,24},{48,32},{56,40},{64,... | collective-permute-start | bytes 442376 | tf_op jit(solution)/shard_map/ppermute | solution.py:372
  73.1 21.4 %all-to-all-start.4 = ((f32[8,2,144,128]{3,2,1,0:T(8,128)}), f32[8,2,144,128]{3,2,1,0:T(8,128)S(1)}, u32[]{:S(2)}, u32[]{:S(2)}) async-start(f32[8,2,144,128]{3,2,1,0:T(8,128)} %bitcast.9), calls=%async_computation.4 | async-start | bytes 2359296 | tf_op jit(solution)/shard_map/all_to_all | solution.py:350
  94.5 85.3 %all-to-all-start.2 = ((f32[32,72,128]{2,1,0:T(8,128)}), f32[32,72,128]{2,1,0:T(8,128)S(1)}, u32[]{:S(2)}, u32[]{:S(2)}) async-start(f32[32,72,128]{2,1,0:T(8,128)} %bitcast.6), calls=%async_computation.2 | async-start | bytes 2359296 | tf_op jit(solution)/shard_map/all_to_all | solution.py:361
  103.2 17.0 %collective-permute-start.11 = (f32[8,72,128]{2,1,0:T(8,128)S(1)}, f32[8,72,128]{2,1,0:T(8,128)S(1)}, u32[]{:S(2)}, u32[]{:S(2)}) collective-permute-start(f32[8,72,128]{2,1,0:T(8,128)S(1)} %get-tuple-element.51), channel_id=1, source_target_pairs={{0,128},{8,136},{16,144},{24,152},{32,160},{40,168},{48,176},{56,1... | collective-permute-start | bytes 884744 | tf_op jit(solution)/shard_map/ppermute | solution.py:368
  103.8 25.9 %collective-permute-start.12 = (f32[8,72,128]{2,1,0:T(8,128)S(1)}, f32[8,72,128]{2,1,0:T(8,128)S(1)}, u32[]{:S(2)}, u32[]{:S(2)}) collective-permute-start(f32[8,72,128]{2,1,0:T(8,128)S(1)} %get-tuple-element.52), channel_id=1, source_target_pairs={{0,136},{8,128},{16,152},{24,144},{32,168},{40,160},{48,184},{56,1... | collective-permute-start | bytes 884744 | tf_op jit(solution)/shard_map/ppermute | solution.py:368
  136.6 19.4 %collective-permute-start.15 = (f32[4,72,128]{2,1,0:T(8,128)S(1)}, f32[4,72,128]{2,1,0:T(8,128)S(1)}, u32[]{:S(2)}, u32[]{:S(2)}) collective-permute-start(f32[4,72,128]{2,1,0:T(8,128)S(1)} %get-tuple-element.55), channel_id=1, source_target_pairs={{0,48},{8,56},{16,64},{24,72},{32,80},{40,88},{48,96},{56,104},{64... | collective-permute-start | bytes 442376 | tf_op jit(solution)/shard_map/ppermute | solution.py:372
  136.6 25.2 %collective-permute-start.16 = (f32[4,72,128]{2,1,0:T(8,128)S(1)}, f32[4,72,128]{2,1,0:T(8,128)S(1)}, u32[]{:S(2)}, u32[]{:S(2)}) collective-permute-start(f32[4,72,128]{2,1,0:T(8,128)S(1)} %get-tuple-element.56), channel_id=1, source_target_pairs={{0,64},{8,72},{16,80},{24,88},{32,96},{40,104},{48,112},{56,120},{... | collective-permute-start | bytes 442376 | tf_op jit(solution)/shard_map/ppermute | solution.py:372
  141.7 20.2 %collective-permute-start.17 = (f32[4,72,128]{2,1,0:T(8,128)S(1)}, f32[4,72,128]{2,1,0:T(8,128)S(1)}, u32[]{:S(2)}, u32[]{:S(2)}) collective-permute-start(f32[4,72,128]{2,1,0:T(8,128)S(1)} %get-tuple-element.57), channel_id=1, source_target_pairs={{0,80},{8,88},{16,96},{24,104},{32,112},{40,120},{48,0},{56,8},{64... | collective-permute-start | bytes 442376 | tf_op jit(solution)/shard_map/ppermute | solution.py:372
  141.8 23.5 %collective-permute-start.18 = (f32[4,72,128]{2,1,0:T(8,128)S(1)}, f32[4,72,128]{2,1,0:T(8,128)S(1)}, u32[]{:S(2)}, u32[]{:S(2)}) collective-permute-start(f32[4,72,128]{2,1,0:T(8,128)S(1)} %get-tuple-element.58), channel_id=1, source_target_pairs={{0,96},{8,104},{16,112},{24,120},{32,0},{40,8},{48,16},{56,24},{64... | collective-permute-start | bytes 442376 | tf_op jit(solution)/shard_map/ppermute | solution.py:372
  145.9 22.6 %collective-permute-start.19 = (f32[4,72,128]{2,1,0:T(8,128)S(1)}, f32[4,72,128]{2,1,0:T(8,128)S(1)}, u32[]{:S(2)}, u32[]{:S(2)}) collective-permute-start(f32[4,72,128]{2,1,0:T(8,128)S(1)} %get-tuple-element.59), channel_id=1, source_target_pairs={{0,112},{8,120},{16,0},{24,8},{32,16},{40,24},{48,32},{56,40},{64,... | collective-permute-start | bytes 442376 | tf_op jit(solution)/shard_map/ppermute | solution.py:372
  179.8 19.8 %all-to-all-start.1 = ((f32[8,2,144,128]{3,2,1,0:T(8,128)}), f32[8,2,144,128]{3,2,1,0:T(8,128)S(1)}, u32[]{:S(2)}, u32[]{:S(2)}) async-start(f32[8,2,144,128]{3,2,1,0:T(8,128)} %bitcast.14), calls=%async_computation.1 | async-start | bytes 2359296 | tf_op jit(solution)/shard_map/all_to_all | solution.py:350
  199.5 78.0 %all-to-all-start.3 = ((f32[8,2,144,128]{3,2,1,0:T(8,128)}), f32[8,2,144,128]{3,2,1,0:T(8,128)S(1)}, u32[]{:S(2)}, u32[]{:S(2)}) async-start(f32[8,2,144,128]{3,2,1,0:T(8,128)} %bitcast.8), calls=%async_computation.3 | async-start | bytes 2359296 | tf_op jit(solution)/shard_map/all_to_all | solution.py:350
  203.2 22.8 %collective-permute-start.1 = (f32[8,72,128]{2,1,0:T(8,128)}, f32[8,72,128]{2,1,0:T(8,128)S(1)}, u32[]{:S(2)}, u32[]{:S(2)}) collective-permute-start(f32[8,72,128]{2,1,0:T(8,128)} %copy-done.16), channel_id=1, source_target_pairs={{0,128},{8,136},{16,144},{24,152},{32,160},{40,168},{48,176},{56,1... | collective-permute-start | bytes 884744 | tf_op jit(solution)/shard_map/ppermute | solution.py:368
  205.5 22.4 %collective-permute-start.2 = (f32[8,72,128]{2,1,0:T(8,128)}, f32[8,72,128]{2,1,0:T(8,128)S(1)}, u32[]{:S(2)}, u32[]{:S(2)}) collective-permute-start(f32[8,72,128]{2,1,0:T(8,128)} %copy-done.15), channel_id=1, source_target_pairs={{0,136},{8,128},{16,152},{24,144},{32,168},{40,160},{48,184},{56,1... | collective-permute-start | bytes 884744 | tf_op jit(solution)/shard_map/ppermute | solution.py:368
  233.8 16.3 %collective-permute-start.5 = (f32[4,72,128]{2,1,0:T(8,128)S(1)}, f32[4,72,128]{2,1,0:T(8,128)S(1)}, u32[]{:S(2)}, u32[]{:S(2)}) collective-permute-start(f32[4,72,128]{2,1,0:T(8,128)S(1)} %get-tuple-element.44), channel_id=1, source_target_pairs={{0,48},{8,56},{16,64},{24,72},{32,80},{40,88},{48,96},{56,104},{64... | collective-permute-start | bytes 442376 | tf_op jit(solution)/shard_map/ppermute | solution.py:372
  236.8 26.4 %collective-permute-start.6 = (f32[4,72,128]{2,1,0:T(8,128)S(1)}, f32[4,72,128]{2,1,0:T(8,128)S(1)}, u32[]{:S(2)}, u32[]{:S(2)}) collective-permute-start(f32[4,72,128]{2,1,0:T(8,128)S(1)} %get-tuple-element.45), channel_id=1, source_target_pairs={{0,64},{8,72},{16,80},{24,88},{32,96},{40,104},{48,112},{56,120},{... | collective-permute-start | bytes 442376 | tf_op jit(solution)/shard_map/ppermute | solution.py:372
  239.8 23.3 %collective-permute-start.7 = (f32[4,72,128]{2,1,0:T(8,128)S(1)}, f32[4,72,128]{2,1,0:T(8,128)S(1)}, u32[]{:S(2)}, u32[]{:S(2)}) collective-permute-start(f32[4,72,128]{2,1,0:T(8,128)S(1)} %get-tuple-element.46), channel_id=1, source_target_pairs={{0,80},{8,88},{16,96},{24,104},{32,112},{40,120},{48,0},{56,8},{64... | collective-permute-start | bytes 442376 | tf_op jit(solution)/shard_map/ppermute | solution.py:372
  244.8 21.7 %collective-permute-start.8 = (f32[4,72,128]{2,1,0:T(8,128)S(1)}, f32[4,72,128]{2,1,0:T(8,128)S(1)}, u32[]{:S(2)}, u32[]{:S(2)}) collective-permute-start(f32[4,72,128]{2,1,0:T(8,128)S(1)} %get-tuple-element.47), channel_id=1, source_target_pairs={{0,96},{8,104},{16,112},{24,120},{32,0},{40,8},{48,16},{56,24},{64... | collective-permute-start | bytes 442376 | tf_op jit(solution)/shard_map/ppermute | solution.py:372
  248.3 18.9 %collective-permute-start.9 = (f32[4,72,128]{2,1,0:T(8,128)S(1)}, f32[4,72,128]{2,1,0:T(8,128)S(1)}, u32[]{:S(2)}, u32[]{:S(2)}) collective-permute-start(f32[4,72,128]{2,1,0:T(8,128)S(1)} %get-tuple-element.48), channel_id=1, source_target_pairs={{0,112},{8,120},{16,0},{24,8},{32,16},{40,24},{48,32},{56,40},{64,... | collective-permute-start | bytes 442376 | tf_op jit(solution)/shard_map/ppermute | solution.py:372
  278.6 23.2 %all-to-all-start = ((f32[8,2,144,128]{3,2,1,0:T(8,128)}), f32[8,2,144,128]{3,2,1,0:T(8,128)S(1)}, u32[]{:S(2)}, u32[]{:S(2)}) async-start(f32[8,2,144,128]{3,2,1,0:T(8,128)} %bitcast.13), calls=%async_computation | async-start | bytes 2359296 | tf_op jit(solution)/shard_map/all_to_all | solution.py:350
  (29 other events, 366.6 us)
where the time goes:
time: 313 us; the launch traced here: 310 us
  waiting for transfers between devices  156 us (50%)
  starting transfers between devices  77.8 us (25%)
  Pallas kernels  61.3 us (20%)
  local copies, waits for them, and re-layouts  14.5 us (5%)
    ppermute x21, waiting for transfers between devices, body(): received[dz - 1] = lax.ppermute(sends[dz - 1], 'gx', shift(0, dz, 0))  69.5 us
    ppermute x9, waiting for transfers between devices, body(): parts.append(lax.ppermute(part, 'gx', shift(dh, 0, dc)))  58 us
    ppermute x21, starting transfers between devices, body(): received[dz - 1] = lax.ppermute(sends[dz - 1], 'gx', shift(0, dz, 0))  41.1 us
    pallas_call x4, Pallas kernels, x_transform(): pl.pallas_call(kernel, grid_spec=pltpu.PrefetchScalarGridSpec(num_scalar_...  37.2 us
    all_to_all x4, waiting for transfers between devices, over_y(): return lax.all_to_all(blocks, 'gy', split_axis=0, concat_axis=0, tiled=True)  28.2 us
    all_to_all x4, starting transfers between devices, over_y(): return lax.all_to_all(blocks, 'gy', split_axis=0, concat_axis=0, tiled=True)  18 us
    unnamed x36, local copies, waits for them, and re-layouts  14.5 us
    pallas_call x2, Pallas kernels, y_transform(): pl.pallas_call(y_kernel, grid=(1,), in_specs=in_specs, out_specs=block, o...  11.1 us
  transfers between devices with their start and end apart: 35, of which 24 were waited for; matrix products, arithmetic and copies ran while one was open for 0% of the time, Pallas kernels for 12%

commit v1 on v0

v1 whole, which is shorter than its diff:
```python
import functools
import math

import jax
import jax.numpy as jnp
import ml_dtypes
import numpy as np
from jax import lax
from jax.experimental import pallas as pl
from jax.experimental.pallas import tpu as pltpu
from jax.sharding import PartitionSpec as P

NX = 2304
NY = 2000
KX = 1152
NQ = 9
STRIP = 72
LANES = 128
ROWS = 250
NJ = 8
NZ = 8
TILE = 16
VMEM = 63 * 1000 * 1000


def split_table(table):
    high = table.astype(np.float32).astype(ml_dtypes.bfloat16)
    low = (table - high.astype(np.float64)).astype(np.float32).astype(ml_dtypes.bfloat16)
    return high, low


@functools.cache
def x_table():
    b = np.arange(LANES)
    steps = []
    for q in range(NQ):
        groups = np.array([0, 9] if q == 0 else [q, 18 - q])
        k = 144 * np.arange(NJ)[:, None, None] + groups[None, :, None] + 18 * np.arange(8)[None, None, :]
        angle = 2.0 * np.pi / NX * ((k[..., None] * b) % NX)
        cosine, sine = np.cos(angle), np.sin(angle)
        rows = np.zeros((NJ, 2, 2, 8, 2, LANES))
        for group in range(2):
            if q == 0:
                rows[:, group, 0, :, group] = cosine[:, group]
                rows[:, group, 1, :, group] = -sine[:, group]
            else:
                sign = 1 - 2 * group
                rows[:, group, 0, :, 0] = cosine[:, group]
                rows[:, group, 0, :, 1] = sign * sine[:, group]
                rows[:, group, 1, :, 0] = -sine[:, group]
                rows[:, group, 1, :, 1] = sign * cosine[:, group]
        steps.append(np.concatenate(split_table(rows.reshape(256, 256) / math.sqrt(NX))))
    return np.stack(steps)


@functools.cache
def y_tables():
    b = np.arange(2 * LANES)
    twist = 2.0 * np.pi / NY * ((np.arange(NJ)[:, None] * b[None, :]) % NY)
    twiddle = np.stack([np.cos(twist), np.sin(twist)], axis=1)
    twiddle = twiddle.reshape(NJ, 2, 2, LANES).transpose(2, 0, 1, 3).astype(np.float32)
    d = np.arange(2 * LANES)
    angle = 2.0 * np.pi / ROWS * ((b[:, None] * d[None, :]) % ROWS)
    keep = ((b < ROWS)[:, None] & (d < ROWS)[None, :]).astype(np.float64) / math.sqrt(NY)
    cosine, sine = np.cos(angle) * keep, np.sin(angle) * keep
    from_real = np.concatenate([cosine, -sine], axis=1)
    from_imag = np.concatenate([sine, cosine], axis=1)
    rows = np.concatenate([from_real[:LANES], from_imag[:LANES], from_real[LANES:], from_imag[LANES:]], axis=0)
    main = np.stack(split_table(rows))
    weave = np.zeros((4, 2 * LANES, 2 * LANES), np.float32)
    for t in range(4):
        for upper in range(2):
            for lane in range(LANES):
                c = 4 * upper + (lane // 32 - t) % 4
                weave[t, upper * LANES + lane, 8 * (lane % 32) + c] = 1.0
    return twiddle, main, weave.astype(ml_dtypes.bfloat16)


LIGHT = pl.CostEstimate(flops=0, bytes_accessed=0, transcendentals=0)


def compiler_params():
    return pltpu.CompilerParams(vmem_limit_bytes=VMEM)


def store_lanes(out, value, half):
    if half == 0:
        out[...] = value
    else:
        out[...] = jnp.zeros(out.shape, out.dtype)
        out[..., : ROWS - LANES] = value


PARTNERS = ((0, 0), (0, 1), (1, 0), (1, 1))


def pack(place, fields, field, after):
    def kernel(place, a, *refs):
        outs = refs[len(after) :]
        if field == 0:
            for hi in range(2):
                for core in range(2):
                    outs[0][hi, :, core, 0] = a[hi, :, core, 0, :, :LANES]
                    store_lanes(outs[0].at[hi, :, core, 1], a[hi, :, core, 0, :, LANES:], 1)
        for half in range(2 * field):
            for i, (dh, dc) in enumerate(PARTNERS):
                to_hi = pl.ds(lax.rem(place[0] + dh, 2), 1)
                to_core = lax.rem(place[2] + dc, 2)
                lanes = slice(0, LANES) if half == 0 else slice(LANES, ROWS)
                for z in range(2):
                    store_lanes(outs[i].at[pl.ds(z, 1)], a[to_hi, z, to_core, 0, :, lanes], half)
            outs = outs[4:]

    parts = 8 * field
    shape = [jax.ShapeDtypeStruct((NZ, STRIP, LANES), jnp.float32)] * parts
    spec = [pl.BlockSpec((2, STRIP, LANES), lambda i, place: (i, 0, 0))] * parts
    if field == 0:
        shape.insert(0, jax.ShapeDtypeStruct((2, NZ, 2, 2, STRIP, LANES), jnp.float32))
        spec.insert(0, pl.BlockSpec((2, 2, 2, 2, STRIP, LANES), lambda i, place: (0, i, 0, 0, 0, 0)))
    return pl.pallas_call(
        kernel,
        grid_spec=pltpu.PrefetchScalarGridSpec(
            num_scalar_prefetch=1,
            grid=(4,),
            in_specs=[pl.BlockSpec((2, 2, 2, 1, STRIP, ROWS), lambda i, place: (0, i, 0, field, 0, 0))]
            + [pl.BlockSpec(memory_space=pl.ANY)] * len(after),
            out_specs=spec,
        ),
        out_shape=shape,
        compiler_params=compiler_params(),
        cost_estimate=LIGHT,
        name="pack",
    )(place, fields, *after)


def pack_z(place, parts, after):
    def kernel(place, *refs):
        sources, outs = refs[:4], refs[-7:]
        for dz in range(1, NZ):
            to_z = lax.rem(place[1] + dz, NZ)
            for i in range(4):
                outs[dz - 1][i] = sources[i][to_z]

    shape = jax.ShapeDtypeStruct((4, STRIP, LANES), jnp.float32)
    anywhere = pl.BlockSpec(memory_space=pl.ANY)
    local = pl.BlockSpec(memory_space=pltpu.VMEM)
    return pl.pallas_call(
        kernel,
        in_specs=[pl.BlockSpec(memory_space=pltpu.SMEM)] + [local] * 4 + [anywhere] * len(after),
        out_specs=[local] * 7,
        out_shape=[shape] * 7,
        compiler_params=compiler_params(),
        cost_estimate=LIGHT,
        name="pack_z",
    )(place, *parts, *after)


def nine_point(v):
    sums = [v[i] + v[9 - i] for i in range(1, 5)]
    differences = [v[i] - v[9 - i] for i in range(1, 5)]
    result = [(v[0] + ((sums[0] + sums[1]) + (sums[2] + sums[3])), None)]
    for m in range(1, 5):
        re, im = v[0], None
        for i in range(1, 5):
            re = re + sums[i - 1] * math.cos(2 * math.pi * i * m / 9)
            if i * m % 9:
                term = differences[i - 1] * -math.sin(2 * math.pi * i * m / 9)
                im = term if im is None else im + term
        result.append((re, im))
    return result


def fold(columns, folded, i, carry):
    at = pl.multiple_of(i * TILE, 8)
    x = []
    for a in range(18):
        tiles = []
        for part in range(TILE // 8):
            tile = 16 * a + 2 * i + part
            tiles.append(columns[lax.div(tile, 9), pl.ds(pl.multiple_of(8 * lax.rem(tile, 9), 8), 8), :])
        x.append(jnp.concatenate(tiles, axis=0))
    pairs = [(x[a], x[a + 9]) if a % 2 == 0 else (x[a + 9], x[a]) for a in range(9)]
    even = nine_point([a + b for a, b in pairs])
    odd = nine_point([a - b for a, b in pairs])
    classes = [(even[0][0], odd[0][0])]
    for c in range(1, NQ):
        if c % 2 == 0:
            classes.append(even[c // 2])
        else:
            re, im = odd[(9 - c) // 2]
            classes.append((re, -im))
    at = pl.multiple_of(i * TILE, TILE)
    for q, values in enumerate(classes):
        for comp, value in enumerate(values):
            rows = pl.ds(LANES * comp + at, TILE)
            high = value.astype(jnp.bfloat16)
            folded[q, rows, :LANES] = high
            folded[q, rows, LANES:] = (value - high.astype(jnp.float32)).astype(jnp.bfloat16)
    return carry


def x_transform(place, pieces, after, weight):
    whole = len(pieces) == 1
    halves = pieces[0].shape[1] if whole else 1

    def kernel(place, *refs):
        sources = refs[: len(pieces)]
        table = refs[len(pieces)]
        out, columns, folded, tables, sems, table_sem = refs[-6:]
        load = pltpu.make_async_copy(table, tables, table_sem)
        copies = [[], []]
        if whole:
            for half in range(halves):
                copies[half].append(pltpu.make_async_copy(sources[0].at[:, half], columns.at[half], sems.at[half]))
        else:
            hi, z, core = place[0], place[1], place[2]
            for i, (dh, dc) in enumerate(PARTNERS):
                from_hi = lax.rem(hi + dh, 2)
                from_core = lax.rem(core + dc, 2)
                for dz in range(NZ):
                    from_z = lax.rem(z + NZ - dz, NZ)
                    source = sources[i].at[z] if dz == 0 else sources[3 + dz].at[i]
                    sender = from_hi * 16 + from_z * 2 + from_core
                    copies[0].append(pltpu.make_async_copy(source, columns.at[0, sender], sems.at[0]))
        for copy in copies[0] + copies[1]:
            copy.start()
        load.start()
        for half in range(halves):
            for copy in copies[half]:
                copy.wait()
            lax.fori_loop(0, LANES // TILE, functools.partial(fold, columns.at[half], folded), 0)
            if half == 0:
                load.wait()
            for q in range(NQ):
                product = jnp.dot(tables[q], folded[q], preferred_element_type=jnp.float32)
                upper, lower = product[:256], product[256:]
                total = upper[:, :LANES] + (upper[:, LANES:] + lower[:, :LANES])
                total = total.reshape(NJ, 2, 2, 8, LANES)
                for group, number in enumerate((0, 9) if q == 0 else (q, 18 - q)):
                    out[:, half, :, number] = total[:, group]

    anywhere = pl.BlockSpec(memory_space=pl.ANY)
    local = pl.BlockSpec(memory_space=pltpu.VMEM)
    shape = (NJ, halves, 2, 18, 8, LANES)
    return pl.pallas_call(
        kernel,
        in_specs=[pl.BlockSpec(memory_space=pltpu.SMEM)] + [anywhere] * (len(pieces) + 1 + len(after)),
        out_specs=local,
        scratch_shapes=[
            pltpu.VMEM((halves, 32, STRIP, LANES), jnp.float32),
            pltpu.VMEM((NQ, 256, 256), jnp.bfloat16),
            pltpu.VMEM((NQ, 512, 256), jnp.bfloat16),
            pltpu.SemaphoreType.DMA((2,)),
            pltpu.SemaphoreType.DMA,
        ],
        out_shape=jax.ShapeDtypeStruct(shape, jnp.float32),
        compiler_params=compiler_params(),
        cost_estimate=pl.CostEstimate(flops=weight, bytes_accessed=0, transcendentals=0),
        name="x_transform",
    )(place, *pieces, jnp.asarray(x_table()), *after)


def eight_point(re, im):
    def add(a, b):
        return a[0] + b[0], a[1] + b[1]

    def sub(a, b):
        return a[0] - b[0], a[1] - b[1]

    def four(v):
        s, d = add(v[0], v[2]), sub(v[0], v[2])
        t, e = add(v[1], v[3]), sub(v[1], v[3])
        turned = e[1], -e[0]
        return add(s, t), add(d, turned), sub(s, t), sub(d, turned)

    values = list(zip(re, im))
    even = four(values[0::2])
    odd = four(values[1::2])
    root = math.sqrt(0.5)
    o1 = (odd[1][0] + odd[1][1]) * root, (odd[1][1] - odd[1][0]) * root
    o2 = odd[2][1], -odd[2][0]
    o3 = (odd[3][1] - odd[3][0]) * root, (odd[3][0] + odd[3][1]) * -root
    odd = odd[0], o1, o2, o3
    return [add(e, o) for e, o in zip(even, odd)] + [sub(e, o) for e, o in zip(even, odd)]


def y_kernel(count, *refs):
    sources = refs[:count]
    twiddle, main, weave = refs[count : count + 3]
    out, gathered, high, low, mixed, woven, sems = refs[-7:]
    copies = []
    for half in range(2):
        source = sources[0].at[:, half] if len(sources) == 1 else sources[half].at[:, 0]
        copies.append(pltpu.make_async_copy(source, gathered.at[half], sems.at[half]))
    for copy in copies:
        copy.start()
    for half in range(2):
        source = gathered.at[half]
        copies[half].wait()

        def fold(i, carry, half=half, source=source):
            rows = pl.ds(pl.multiple_of(i * TILE, TILE), TILE)
            re = [source[j, 0, rows, :] for j in range(NJ)]
            im = [source[j, 1, rows, :] for j in range(NJ)]
            for c, (a, b) in enumerate(eight_point(re, im)):
                if c > 0:
                    cosine = twiddle[half, c, 0:1, :]
                    sine = twiddle[half, c, 1:2, :]
                    a, b = a * cosine + b * sine, b * cosine - a * sine
                for comp, value in enumerate((a, b)):
                    lanes = slice((2 * half + comp) * LANES, (2 * half + comp + 1) * LANES)
                    top = value.astype(jnp.bfloat16)
                    high[c, rows, lanes] = top
                    low[c, rows, lanes] = (value - top.astype(jnp.float32)).astype(jnp.bfloat16)
            return carry

        lax.fori_loop(0, 144 // TILE, fold, 0)

    for c in range(NJ):
        a = high[c]
        value = (
            jnp.dot(a, main[0], preferred_element_type=jnp.float32)
            + jnp.dot(low[c], main[0], preferred_element_type=jnp.float32)
            + jnp.dot(a, main[1], preferred_element_type=jnp.float32)
        )
        for part in range(4):
            piece = value[:, part * LANES : (part + 1) * LANES]
            if c % 4 > 0:
                piece = pltpu.roll(piece, 32 * (c % 4), 1)
            for group in range(18):
                mixed[c, part, pl.ds(group, 8, stride=18), :] = piece[8 * group : 8 * group + 8]

    slot = lax.broadcasted_iota(jnp.int32, (144, LANES), 1) // 32
    for t in range(4):
        for comp in range(2):
            for upper in range(2):
                part = 2 * comp + upper
                for group in range(2):
                    value = mixed[4 * group, part]
                    for c in range(1, 4):
                        value = jnp.where(slot == (c + t) % 4, mixed[4 * group + c, part], value)
                    top = value.astype(jnp.bfloat16)
                    start = part * 144
                    columns = slice(group * LANES, (group + 1) * LANES)
                    woven[start : start + 144, columns] = top
                    woven[start + 576 : start + 720, columns] = (value - top.astype(jnp.float32)).astype(jnp.bfloat16)
        product = jnp.dot(woven[...], weave[t], preferred_element_type=jnp.float32)
        product = product[:576] + product[576:]
        for comp in range(2):
            for upper in range(2):
                tile = 4 * upper + t
                width = min(256, NY - 256 * tile)
                start = (2 * comp + upper) * 144
                out[comp, 0, :, 256 * tile : 256 * tile + width] = product[start : start + 144, :width]


def y_transform(field, arrays, before):
    twiddle, main, weave = y_tables()
    anywhere = pl.BlockSpec(memory_space=pl.ANY)
    local = pl.BlockSpec(memory_space=pltpu.VMEM)
    inputs = [*arrays, jnp.asarray(twiddle), jnp.asarray(main), jnp.asarray(weave)]
    in_specs = [anywhere] * len(arrays) + [local] * 3
    aliases = {}
    if before is not None:
        aliases = {len(inputs): 0}
        inputs.append(before)
        in_specs.append(anywhere)
    return pl.pallas_call(
        functools.partial(y_kernel, len(arrays)),
        grid=(1,),
        in_specs=in_specs,
        out_specs=pl.BlockSpec((2, 1, 144, NY), lambda i: (0, field, 0, 0)),
        out_shape=jax.ShapeDtypeStruct((2, 2, 144, NY), jnp.float32),
        scratch_shapes=[
            pltpu.VMEM((2, NJ, 2, 144, LANES), jnp.float32),
            pltpu.VMEM((NJ, 144, 512), jnp.bfloat16),
            pltpu.VMEM((NJ, 144, 512), jnp.bfloat16),
            pltpu.VMEM((NJ, 4, 144, LANES), jnp.float32),
            pltpu.VMEM((1152, 256), jnp.bfloat16),
            pltpu.SemaphoreType.DMA((2,)),
        ],
        input_output_aliases=aliases,
        compiler_params=compiler_params(),
        cost_estimate=LIGHT,
        name="y_transform",
    )(*inputs)


def shift(dh, dz, dc):
    pairs = []
    for hi in range(2):
        for z in range(NZ):
            for core in range(2):
                to = (hi + dh) % 2 * 16 + (z + dz) % NZ * 2 + (core + dc) % 2
                pairs.append((hi * 16 + z * 2 + core, to))
    return pairs


def over_y(blocks):
    blocks = blocks.reshape(NJ, -1, 2, 144, LANES)
    return lax.all_to_all(blocks, "gy", split_axis=0, concat_axis=0, tiled=True)


def over_xh(parts):
    return parts[:1] + [lax.ppermute(part, "gx", shift(dh, 0, dc)) for (dh, dc), part in zip(PARTNERS[1:], parts[1:])]


def over_z(sends, order):
    return {dz: lax.ppermute(sends[dz - 1], "gx", shift(0, dz, 0)) for dz in order}


def listed(received):
    return [received[dz] for dz in range(1, NZ)]


def body(fields):
    me = lax.axis_index("gx")
    place = jnp.stack([me // 16, me // 2 % NZ, me % 2]).astype(jnp.int32)
    fields = fields.reshape(2, NZ, 2, 2, STRIP, ROWS)
    first = pack(place, fields, 0, [])[0]
    rest = list(pack(place, fields, 1, [first]))
    first = first.reshape(32, 2, STRIP, LANES)
    first = lax.all_to_all(first, "gx", split_axis=0, concat_axis=0, tiled=True)
    parts = [over_xh(rest[:4]), over_xh(rest[4:])]
    sends = [list(pack_z(place, part, [])) for part in parts]
    second = over_z(sends[0], (1, 7, 2, 6))
    first, sends, second = lax.optimization_barrier((first, sends, second))
    x01 = x_transform(place, [first], [], 2 * 10**10)
    x01, sends = lax.optimization_barrier((x01, sends))
    g01 = over_y(x01)
    second |= over_z(sends[0], (4, 3, 5))
    flying = over_z(sends[1], (4, 2, 6))
    third = over_z(sends[1], (3, 5, 1, 7))
    x2 = x_transform(place, parts[0] + listed(second), [], 2 * 10**10)
    x2, flying = lax.optimization_barrier((x2, flying))
    third |= flying
    g01, x2 = lax.optimization_barrier((g01, x2))
    g2 = over_y(x2)
    x3 = x_transform(place, parts[1] + listed(third), [x2], 2 * 10**11)
    g2, x3 = lax.optimization_barrier((g2, x3))
    g3 = over_y(x3)
    result = y_transform(0, [g01], None)
    return y_transform(1, [g2, g3], result)


def solution(mesh):
    in_specs = (P(None, "gx", "gy"),)
    out_specs = P(None, "gx", "gy", None)
    return jax.shard_map(body, mesh=mesh, in_specs=in_specs, out_specs=out_specs, check_vma=False)
```

time: 313 us -> 188 us (0.60)
  waiting for transfers between devices: 156 us -> 60.9 us
  Pallas kernels: 61.3 us -> 49.5 us
  local copies, waits for them, and re-layouts: 14.5 us -> 4.57 us
  starting transfers between devices: 77.8 us -> 71.5 us
    ppermute x30 -> x20, waiting for transfers between devices: 127 us -> 49.1 us  [the longest x6 31.6 us: over_xh(): lax.ppermute(part, 'gx', shift(dh, 0, dc))]
    all_to_all x4 -> x3, waiting for transfers between devices: 28.2 us -> 11.8 us  [over_y(): return lax.all_to_all(blocks, 'gy', split_axis=0, concat_axis=0, tiled=True)]
    pallas_call x8 -> x7, Pallas kernels: 55.4 us -> 44.9 us  [the longest x3 19.1 us: x_transform(): pl.pallas_call(kernel, in_specs=[pl.BlockSpec(memory_space=pltpu.SMEM)] +...]
    unnamed x36 -> x48, local copies, waits for them, and re-layouts: 14.5 us -> 4.57 us
    ppermute x30 -> x20, starting transfers between devices: 51.3 us -> 43 us  [the longest x14 36.2 us: over_z(): lax.ppermute(sends[dz - 1], 'gx', shift(0, dz, 0))]
    all_to_all x4 -> x3, starting transfers between devices: 18 us -> 17.9 us  [over_y(): return lax.all_to_all(blocks, 'gy', split_axis=0, concat_axis=0, tiled=True)]
  transfers between devices with their start and end apart: 35 -> 24, of which waited for: 24 -> 11; matrix products, arithmetic and copies ran while one was open for 0% -> 0% of each run, Pallas kernels for 12% -> 15%
where the time goes in v1:
time: 188 us
  starting transfers between devices  71.5 us (38%)
  waiting for transfers between devices  60.9 us (32%)
  Pallas kernels  49.5 us (26%)
  local copies, waits for them, and re-layouts  4.57 us (2%)
    ppermute x14, starting transfers between devices, over_z(): lax.ppermute(sends[dz - 1], 'gx', shift(0, dz, 0))  36.2 us
    ppermute x6, waiting for transfers between devices, over_xh(): lax.ppermute(part, 'gx', shift(dh, 0, dc))  31.6 us
    pallas_call x3, Pallas kernels, x_transform(): pl.pallas_call(kernel, in_specs=[pl.BlockSpec(memory_space=pltpu.SMEM)] +...  19.1 us
    all_to_all x3, starting transfers between devices, over_y(): return lax.all_to_all(blocks, 'gy', split_axis=0, concat_axis=0, tiled=True)  17.9 us
    ppermute x14, waiting for transfers between devices, over_z(): lax.ppermute(sends[dz - 1], 'gx', shift(0, dz, 0))  17.4 us
    pallas_call x2, Pallas kernels, y_transform(): pl.pallas_call(functools.partial(y_kernel, len(arrays)), grid=(1,), in_sp...  16.5 us
    all_to_all x3, waiting for transfers between devices, over_y(): return lax.all_to_all(blocks, 'gy', split_axis=0, concat_axis=0, tiled=True)  11.8 us
    all_to_all x1, starting transfers between devices, body(): first = lax.all_to_all(first, 'gx', split_axis=0, concat_axis=0, tiled=True)  10.7 us
  transfers between devices with their start and end apart: 24, of which 11 were waited for; matrix products, arithmetic and copies ran while one was open for 0% of the time, Pallas kernels for 15%

profile of v1, /device:TPU:68, one launch (start us, length us, event | category | flops | bytes accessed | tf_op | source)
XLA Modules:
  0.0 187.6 jit_solution(17069116463409370504)
XLA Ops:
  0.6 4.6 %pack.2.refs_0_ = f32[2,8,2,2,72,128]{5,4,3,2,1,0:T(8,128)} custom-call(s32[3]{0:T(128)} %pad_add_fusion.place, f32[2,8,2,2,72,250]{5,4,3,2,1,0:T(8,128)} %bitcast.9), custom_call_target="tpu_custom_call" | custom-call | tf_op jit(solution)/shard_map/pack/pallas_call | solution.py:120
  5.2 10.7 %all-to-all-start = ((f32[32,2,72,128]{3,2,1,0:T(8,128)}), f32[32,2,72,128]{3,2,1,0:T(8,128)S(1)}, u32[]{:S(2)}, u32[]{:S(2)}) async-start(f32[32,2,72,128]{3,2,1,0:T(8,128)} %bitcast.8), calls=%async_computation | async-start | bytes 4718592 | tf_op jit(solution)/shard_map/all_to_all | solution.py:423
  15.9 4.7 %pack.3 = (f32[8,72,128]{2,1,0:T(8,128)}, f32[8,72,128]{2,1,0:T(8,128)}, f32[8,72,128]{2,1,0:T(8,128)}, f32[8,72,128]{2,1,0:T(8,128)}, f32[8,72,128]{2,1,0:T(8,1...) custom-call(s32[3]{0:T(128)} %pad_add_fusion.place, f32[2,8,2,2,72,250]{5,4,3,2,1,0:T(8,128)} %bitcast.10, ...), custom_call_target="tpu_custom_call" | custom-call | tf_op jit(solution)/shard_map/pack/pallas_call | solution.py:120
  27.4 9.1 %collective-permute-done.1.refs_2_ = f32[8,72,128]{2,1,0:T(8,128)S(1)} collective-permute-done((f32[8,72,128]{2,1,0:T(8,128)}, f32[8,72,128]{2,1,0:T(8,128)S(1)}, u32[]{:S(2)}, u32[]{:S(2)}) %collective-permute-start.1) | collective-permute-done | bytes 294944 | tf_op jit(solution)/shard_map/ppermute | solution.py:405
  36.5 12.5 %collective-permute-done.2.refs_3_ = f32[8,72,128]{2,1,0:T(8,128)} collective-permute-done((f32[8,72,128]{2,1,0:T(8,128)}, f32[8,72,128]{2,1,0:T(8,128)}, u32[]{:S(2)}, u32[]{:S(2)}) %collective-permute-start.2) | collective-permute-done | bytes 294944 | tf_op jit(solution)/shard_map/ppermute | solution.py:405
  62.4 7.1 %collective-permute-done.5.refs_3_ = f32[8,72,128]{2,1,0:T(8,128)S(1)} collective-permute-done((f32[8,72,128]{2,1,0:T(8,128)}, f32[8,72,128]{2,1,0:T(8,128)S(1)}, u32[]{:S(2)}, u32[]{:S(2)}) %collective-permute-start.5) | collective-permute-done | bytes 294944 | tf_op jit(solution)/shard_map/ppermute | solution.py:405
  72.5 3.9 %collective-permute-done.7.refs_5_ = f32[4,72,128]{2,1,0:T(8,128)S(1)} collective-permute-done((f32[4,72,128]{2,1,0:T(8,128)}, f32[4,72,128]{2,1,0:T(8,128)S(1)}, u32[]{:S(2)}, u32[]{:S(2)}) %collective-permute-start.7) | collective-permute-done | bytes 147488 | tf_op jit(solution)/shard_map/ppermute | solution.py:409
  80.0 8.4 %x_transform.3 = f32[8,2,2,18,8,128]{5,4,3,2,1,0:T(8,128)} custom-call(s32[3]{0:T(128)} %pad_add_fusion.place, f32[32,2,72,128]{3,2,1,0:T(8,128)} %copy-done.2, bf16[9,512,256]{2,1,0:T(8,128)(2,1)} %constant.59.clone.refs_1_.refs_11_), custom_call_target="tpu_custom_call" | custom-call | flops 20000000000 | tf_op jit(solution)/shard_map/x_transform/pallas_call | solution.py:245
  88.5 5.2 %all-to-all-start.1 = ((f32[8,2,2,144,128]{4,3,2,1,0:T(8,128)}), f32[8,2,2,144,128]{4,3,2,1,0:T(8,128)S(1)}, u32[]{:S(2)}, u32[]{:S(2)}) async-start(f32[8,2,2,144,128]{4,3,2,1,0:T(8,128)} %bitcast.11), calls=%async_computation.1 | async-start | bytes 4718592 | tf_op jit(solution)/shard_map/all_to_all | solution.py:401
  93.7 4.1 %collective-permute-start.10 = (f32[4,72,128]{2,1,0:T(8,128)}, f32[4,72,128]{2,1,0:T(8,128)S(1)}, u32[]{:S(2)}, u32[]{:S(2)}) collective-permute-start(f32[4,72,128]{2,1,0:T(8,128)} %get-tuple-element.97), channel_id=1, source_target_pairs={{0,48},{8,56},{16,64},{24,72},{32,80},{40,88},{48,96},{56,104},{64... | collective-permute-start | bytes 442376 | tf_op jit(solution)/shard_map/ppermute | solution.py:409
  100.6 3.2 %collective-permute-start.12 = (f32[4,72,128]{2,1,0:T(8,128)S(1)}, f32[4,72,128]{2,1,0:T(8,128)S(1)}, u32[]{:S(2)}, u32[]{:S(2)}) collective-permute-start(f32[4,72,128]{2,1,0:T(8,128)S(1)} %copy-done.16), channel_id=1, source_target_pairs={{0,80},{8,88},{16,96},{24,104},{32,112},{40,120},{48,0},{56,8},{64... | collective-permute-start | bytes 442376 | tf_op jit(solution)/shard_map/ppermute | solution.py:409
  104.3 3.1 %collective-permute-start.14 = (f32[4,72,128]{2,1,0:T(8,128)}, f32[4,72,128]{2,1,0:T(8,128)}, u32[]{:S(2)}, u32[]{:S(2)}) collective-permute-start(f32[4,72,128]{2,1,0:T(8,128)} %get-tuple-element.103), channel_id=1, source_target_pairs={{0,64},{8,72},{16,80},{24,88},{32,96},{40,104},{48,112},{56,120},{... | collective-permute-start | bytes 442376 | tf_op jit(solution)/shard_map/ppermute | solution.py:409
  107.4 3.6 %collective-permute-done.10.refs_6_ = f32[4,72,128]{2,1,0:T(8,128)S(1)} collective-permute-done((f32[4,72,128]{2,1,0:T(8,128)}, f32[4,72,128]{2,1,0:T(8,128)S(1)}, u32[]{:S(2)}, u32[]{:S(2)}) %collective-permute-start.10) | collective-permute-done | bytes 147488 | tf_op jit(solution)/shard_map/ppermute | solution.py:409
  111.2 7.7 %collective-permute-done.11.refs_7_ = f32[4,72,128]{2,1,0:T(8,128)S(1)} collective-permute-done((f32[4,72,128]{2,1,0:T(8,128)S(1)}, f32[4,72,128]{2,1,0:T(8,128)S(1)}, u32[]{:S(2)}, u32[]{:S(2)}) %collective-permute-start.11) | collective-permute-done | bytes 147488 | tf_op jit(solution)/shard_map/ppermute | solution.py:409
  118.9 8.5 %collective-permute-start.17 = (f32[4,72,128]{2,1,0:T(8,128)S(1)}, f32[4,72,128]{2,1,0:T(8,128)S(1)}, u32[]{:S(2)}, u32[]{:S(2)}) collective-permute-start(f32[4,72,128]{2,1,0:T(8,128)S(1)} %copy-done.12), channel_id=1, source_target_pairs={{0,48},{8,56},{16,64},{24,72},{32,80},{40,88},{48,96},{56,104},{64... | collective-permute-start | bytes 442376 | tf_op jit(solution)/shard_map/ppermute | solution.py:409
  128.1 5.7 %collective-permute-start.19 = (f32[4,72,128]{2,1,0:T(8,128)S(1)}, f32[4,72,128]{2,1,0:T(8,128)}, u32[]{:S(2)}, u32[]{:S(2)}) collective-permute-start(f32[4,72,128]{2,1,0:T(8,128)S(1)} %copy-done.9), channel_id=1, source_target_pairs={{0,112},{8,120},{16,0},{24,8},{32,16},{40,24},{48,32},{56,40},{64,... | collective-permute-start | bytes 442376 | tf_op jit(solution)/shard_map/ppermute | solution.py:409
  133.8 5.3 %x_transform.4.refs_12_ = f32[8,1,2,18,8,128]{5,4,3,2,1,0:T(8,128)} custom-call(s32[3]{0:T(128)} %pad_add_fusion.place, f32[8,72,128]{2,1,0:T(8,128)} %get-tuple-element.61.refs_0_, f32[8,72,128]{2,1,0:T(8,128)} %copy-done.6, f32[8,72,128]{2,1,0:T(8,128)} %copy-done.7, f32[8,72,128]{2,1,0:T(8,128)} %collective-permute-done.2.refs_3_, ...), custom_call_target="tpu_custom_call" | custom-call | flops 20000000000 | tf_op jit(solution)/shard_map/x_transform/pallas_call | solution.py:245
  139.2 7.1 %all-to-all-start.2 = ((f32[8,1,2,144,128]{4,3,2,1,0:T(8,128)}), f32[8,1,2,144,128]{4,3,2,1,0:T(8,128)}, u32[]{:S(2)}, u32[]{:S(2)}) async-start(f32[8,1,2,144,128]{4,3,2,1,0:T(8,128)} %bitcast.12), calls=%async_computation.2 | async-start | bytes 2359296 | tf_op jit(solution)/shard_map/all_to_all | solution.py:401
  147.0 5.4 %x_transform.5 = f32[8,1,2,18,8,128]{5,4,3,2,1,0:T(8,128)} custom-call(s32[3]{0:T(128)} %pad_add_fusion.place, f32[8,72,128]{2,1,0:T(8,128)} %get-tuple-element.72.refs_0_, f32[8,72,128]{2,1,0:T(8,128)} %copy-done.3, f32[8,72,128]{2,1,0:T(8,128)} %copy-done.4, f32[8,72,128]{2,1,0:T(8,128)} %copy-done.5, f32[4,72,128]{2,1,0:T(8,128)} %copy-done.19, ...), custom_call_target="tpu_custom_call" | custom-call | flops 199999995904 | tf_op jit(solution)/shard_map/x_transform/pallas_call | solution.py:245
  152.4 7.9 %all-to-all-done.2.refs_0_ = f32[8,1,2,144,128]{4,3,2,1,0:T(8,128)} async-done(((f32[8,1,2,144,128]{4,3,2,1,0:T(8,128)}), f32[8,1,2,144,128]{4,3,2,1,0:T(8,128)}, u32[]{:S(2)}, u32[]{:S(2)}) %all-to-all-start.2) | async-done | bytes 1179680 | tf_op jit(solution)/shard_map/all_to_all | solution.py:401
  160.3 5.5 %all-to-all-start.3 = ((f32[8,1,2,144,128]{4,3,2,1,0:T(8,128)}), f32[8,1,2,144,128]{4,3,2,1,0:T(8,128)S(1)}, u32[]{:S(2)}, u32[]{:S(2)}) async-start(f32[8,1,2,144,128]{4,3,2,1,0:T(8,128)} %bitcast.13), calls=%async_computation.3 | async-start | bytes 2359296 | tf_op jit(solution)/shard_map/all_to_all | solution.py:401
  165.8 8.3 %y_transform.2.refs_5_ = f32[2,2,144,2000]{3,2,1,0:T(8,128)} custom-call(f32[8,2,2,144,128]{4,3,2,1,0:T(8,128)} %copy-done, f32[2,8,2,128]{3,2,1,0:T(2,128)} %constant.60.clone.refs_1_.refs_2_, bf16[2,512,512]{2,1,0:T(8,128)(2,1)} %constant.61.clone.refs_2_.refs_3_, bf16[4,256,256]{2,1,0:T(8,128)(2,1)} %constant.62.clone.refs_3_.refs_4_), custom_call_target="tpu_custom_call" | custom-call | tf_op jit(solution)/shard_map/y_transform/pallas_call | solution.py:368
  174.1 4.0 %all-to-all-done.3.refs_1_ = f32[8,1,2,144,128]{4,3,2,1,0:T(8,128)S(1)} async-done(((f32[8,1,2,144,128]{4,3,2,1,0:T(8,128)}), f32[8,1,2,144,128]{4,3,2,1,0:T(8,128)S(1)}, u32[]{:S(2)}, u32[]{:S(2)}) %all-to-all-start.3) | async-done | bytes 1179680 | tf_op jit(solution)/shard_map/all_to_all | solution.py:401
  179.1 8.3 %y_transform.3 = f32[2,2,144,2000]{3,2,1,0:T(8,128)} custom-call(f32[8,1,2,144,128]{4,3,2,1,0:T(8,128)} %all-to-all-done.2.refs_0_, f32[8,1,2,144,128]{4,3,2,1,0:T(8,128)} %copy-done.1, f32[2,8,2,128]{3,2,1,0:T(2,128)} %constant.60.clone.refs_1_.refs_2_, bf16[2,512,512]{2,1,0:T(8,128)(2,1)} %constant.61.clone.refs_2_.refs_3_, ...), custom_call_target="tpu_custom_call", output_to_operand_aliasing={{}: (5, {})} | custom-call | tf_op jit(solution)/shard_map/y_transform/pallas_call | solution.py:368
  (82 shorter events, 33.2 us)
Async XLA Ops:
  5.2 73.4 %all-to-all-start = ((f32[32,2,72,128]{3,2,1,0:T(8,128)}), f32[32,2,72,128]{3,2,1,0:T(8,128)S(1)}, u32[]{:S(2)}, u32[]{:S(2)}) async-start(f32[32,2,72,128]{3,2,1,0:T(8,128)} %bitcast.8), calls=%async_computation | async-start | bytes 4718592 | tf_op jit(solution)/shard_map/all_to_all | solution.py:423
  20.6 4.4 %collective-permute-start = (f32[8,72,128]{2,1,0:T(8,128)}, f32[8,72,128]{2,1,0:T(8,128)S(1)}, u32[]{:S(2)}, u32[]{:S(2)}) collective-permute-start(f32[8,72,128]{2,1,0:T(8,128)} %get-tuple-element.62), channel_id=1, source_target_pairs={{0,8},{8,0},{16,24},{24,16},{32,40},{40,32},{48,56},{56,48},{64,72... | collective-permute-start | bytes 884744 | tf_op jit(solution)/shard_map/ppermute | solution.py:405
  20.8 15.7 %collective-permute-start.1 = (f32[8,72,128]{2,1,0:T(8,128)}, f32[8,72,128]{2,1,0:T(8,128)S(1)}, u32[]{:S(2)}, u32[]{:S(2)}) collective-permute-start(f32[8,72,128]{2,1,0:T(8,128)} %get-tuple-element.63), channel_id=1, source_target_pairs={{0,128},{8,136},{16,144},{24,152},{32,160},{40,168},{48,176},{56,1... | collective-permute-start | bytes 884744 | tf_op jit(solution)/shard_map/ppermute | solution.py:405
  21.4 27.6 %collective-permute-start.2 = (f32[8,72,128]{2,1,0:T(8,128)}, f32[8,72,128]{2,1,0:T(8,128)}, u32[]{:S(2)}, u32[]{:S(2)}) collective-permute-start(f32[8,72,128]{2,1,0:T(8,128)} %get-tuple-element.64), channel_id=1, source_target_pairs={{0,136},{8,128},{16,152},{24,144},{32,168},{40,160},{48,184},{56,1... | collective-permute-start | bytes 884744 | tf_op jit(solution)/shard_map/ppermute | solution.py:405
  24.1 33.2 %collective-permute-start.3 = (f32[8,72,128]{2,1,0:T(8,128)}, f32[8,72,128]{2,1,0:T(8,128)S(1)}, u32[]{:S(2)}, u32[]{:S(2)}) collective-permute-start(f32[8,72,128]{2,1,0:T(8,128)} %get-tuple-element.73), channel_id=1, source_target_pairs={{0,8},{8,0},{16,24},{24,16},{32,40},{40,32},{48,56},{56,48},{64,72... | collective-permute-start | bytes 884744 | tf_op jit(solution)/shard_map/ppermute | solution.py:405
  24.5 35.7 %collective-permute-start.4 = (f32[8,72,128]{2,1,0:T(8,128)}, f32[8,72,128]{2,1,0:T(8,128)S(1)}, u32[]{:S(2)}, u32[]{:S(2)}) collective-permute-start(f32[8,72,128]{2,1,0:T(8,128)} %get-tuple-element.74), channel_id=1, source_target_pairs={{0,128},{8,136},{16,144},{24,152},{32,160},{40,168},{48,176},{56,1... | collective-permute-start | bytes 884744 | tf_op jit(solution)/shard_map/ppermute | solution.py:405
  25.1 44.4 %collective-permute-start.5 = (f32[8,72,128]{2,1,0:T(8,128)}, f32[8,72,128]{2,1,0:T(8,128)S(1)}, u32[]{:S(2)}, u32[]{:S(2)}) collective-permute-start(f32[8,72,128]{2,1,0:T(8,128)} %get-tuple-element.75), channel_id=1, source_target_pairs={{0,136},{8,128},{16,152},{24,144},{32,168},{40,160},{48,184},{56,1... | collective-permute-start | bytes 884744 | tf_op jit(solution)/shard_map/ppermute | solution.py:405
  51.4 21.2 %collective-permute-start.6 = (f32[4,72,128]{2,1,0:T(8,128)}, f32[4,72,128]{2,1,0:T(8,128)S(1)}, u32[]{:S(2)}, u32[]{:S(2)}) collective-permute-start(f32[4,72,128]{2,1,0:T(8,128)} %get-tuple-element.65), channel_id=1, source_target_pairs={{0,16},{8,24},{16,32},{24,40},{32,48},{40,56},{48,64},{56,72},{64,... | collective-permute-start | bytes 442376 | tf_op jit(solution)/shard_map/ppermute | solution.py:409
  54.4 22.0 %collective-permute-start.7 = (f32[4,72,128]{2,1,0:T(8,128)}, f32[4,72,128]{2,1,0:T(8,128)S(1)}, u32[]{:S(2)}, u32[]{:S(2)}) collective-permute-start(f32[4,72,128]{2,1,0:T(8,128)} %get-tuple-element.66), channel_id=1, source_target_pairs={{0,32},{8,40},{16,48},{24,56},{32,64},{40,72},{48,80},{56,88},{64,... | collective-permute-start | bytes 442376 | tf_op jit(solution)/shard_map/ppermute | solution.py:409
  57.2 20.7 %collective-permute-start.8 = (f32[4,72,128]{2,1,0:T(8,128)}, f32[4,72,128]{2,1,0:T(8,128)S(1)}, u32[]{:S(2)}, u32[]{:S(2)}) collective-permute-start(f32[4,72,128]{2,1,0:T(8,128)} %get-tuple-element.70), channel_id=1, source_target_pairs={{0,96},{8,104},{16,112},{24,120},{32,0},{40,8},{48,16},{56,24},{64... | collective-permute-start | bytes 442376 | tf_op jit(solution)/shard_map/ppermute | solution.py:409
  60.2 18.4 %collective-permute-start.9 = (f32[4,72,128]{2,1,0:T(8,128)}, f32[4,72,128]{2,1,0:T(8,128)}, u32[]{:S(2)}, u32[]{:S(2)}) collective-permute-start(f32[4,72,128]{2,1,0:T(8,128)} %get-tuple-element.71), channel_id=1, source_target_pairs={{0,112},{8,120},{16,0},{24,8},{32,16},{40,24},{48,32},{56,40},{64,... | collective-permute-start | bytes 442376 | tf_op jit(solution)/shard_map/ppermute | solution.py:409
  88.5 50.7 %all-to-all-start.1 = ((f32[8,2,2,144,128]{4,3,2,1,0:T(8,128)}), f32[8,2,2,144,128]{4,3,2,1,0:T(8,128)S(1)}, u32[]{:S(2)}, u32[]{:S(2)}) async-start(f32[8,2,2,144,128]{4,3,2,1,0:T(8,128)} %bitcast.11), calls=%async_computation.1 | async-start | bytes 4718592 | tf_op jit(solution)/shard_map/all_to_all | solution.py:401
  93.7 17.3 %collective-permute-start.10 = (f32[4,72,128]{2,1,0:T(8,128)}, f32[4,72,128]{2,1,0:T(8,128)S(1)}, u32[]{:S(2)}, u32[]{:S(2)}) collective-permute-start(f32[4,72,128]{2,1,0:T(8,128)} %get-tuple-element.97), channel_id=1, source_target_pairs={{0,48},{8,56},{16,64},{24,72},{32,80},{40,88},{48,96},{56,104},{64... | collective-permute-start | bytes 442376 | tf_op jit(solution)/shard_map/ppermute | solution.py:409
  97.9 21.0 %collective-permute-start.11 = (f32[4,72,128]{2,1,0:T(8,128)S(1)}, f32[4,72,128]{2,1,0:T(8,128)S(1)}, u32[]{:S(2)}, u32[]{:S(2)}) collective-permute-start(f32[4,72,128]{2,1,0:T(8,128)S(1)} %copy-done.17), channel_id=1, source_target_pairs={{0,64},{8,72},{16,80},{24,88},{32,96},{40,104},{48,112},{56,120},{... | collective-permute-start | bytes 442376 | tf_op jit(solution)/shard_map/ppermute | solution.py:409
  100.6 18.2 %collective-permute-start.12 = (f32[4,72,128]{2,1,0:T(8,128)S(1)}, f32[4,72,128]{2,1,0:T(8,128)S(1)}, u32[]{:S(2)}, u32[]{:S(2)}) collective-permute-start(f32[4,72,128]{2,1,0:T(8,128)S(1)} %copy-done.16), channel_id=1, source_target_pairs={{0,80},{8,88},{16,96},{24,104},{32,112},{40,120},{48,0},{56,8},{64... | collective-permute-start | bytes 442376 | tf_op jit(solution)/shard_map/ppermute | solution.py:409
  103.9 23.5 %collective-permute-start.13 = (f32[4,72,128]{2,1,0:T(8,128)}, f32[4,72,128]{2,1,0:T(8,128)S(1)}, u32[]{:S(2)}, u32[]{:S(2)}) collective-permute-start(f32[4,72,128]{2,1,0:T(8,128)} %get-tuple-element.102), channel_id=1, source_target_pairs={{0,32},{8,40},{16,48},{24,56},{32,64},{40,72},{48,80},{56,88},{64,... | collective-permute-start | bytes 442376 | tf_op jit(solution)/shard_map/ppermute | solution.py:409
  104.3 23.8 %collective-permute-start.14 = (f32[4,72,128]{2,1,0:T(8,128)}, f32[4,72,128]{2,1,0:T(8,128)}, u32[]{:S(2)}, u32[]{:S(2)}) collective-permute-start(f32[4,72,128]{2,1,0:T(8,128)} %get-tuple-element.103), channel_id=1, source_target_pairs={{0,64},{8,72},{16,80},{24,88},{32,96},{40,104},{48,112},{56,120},{... | collective-permute-start | bytes 442376 | tf_op jit(solution)/shard_map/ppermute | solution.py:409
  111.1 28.2 %collective-permute-start.15 = (f32[4,72,128]{2,1,0:T(8,128)S(1)}, f32[4,72,128]{2,1,0:T(8,128)}, u32[]{:S(2)}, u32[]{:S(2)}) collective-permute-start(f32[4,72,128]{2,1,0:T(8,128)S(1)} %copy-done.15), channel_id=1, source_target_pairs={{0,96},{8,104},{16,112},{24,120},{32,0},{40,8},{48,16},{56,24},{64... | collective-permute-start | bytes 442376 | tf_op jit(solution)/shard_map/ppermute | solution.py:409
  118.9 27.5 %collective-permute-start.16 = (f32[4,72,128]{2,1,0:T(8,128)S(1)}, f32[4,72,128]{2,1,0:T(8,128)S(1)}, u32[]{:S(2)}, u32[]{:S(2)}) collective-permute-start(f32[4,72,128]{2,1,0:T(8,128)S(1)} %copy-done.13), channel_id=1, source_target_pairs={{0,16},{8,24},{16,32},{24,40},{32,48},{40,56},{48,64},{56,72},{64,... | collective-permute-start | bytes 442376 | tf_op jit(solution)/shard_map/ppermute | solution.py:409
  118.9 27.5 %collective-permute-start.17 = (f32[4,72,128]{2,1,0:T(8,128)S(1)}, f32[4,72,128]{2,1,0:T(8,128)S(1)}, u32[]{:S(2)}, u32[]{:S(2)}) collective-permute-start(f32[4,72,128]{2,1,0:T(8,128)S(1)} %copy-done.12), channel_id=1, source_target_pairs={{0,48},{8,56},{16,64},{24,72},{32,80},{40,88},{48,96},{56,104},{64... | collective-permute-start | bytes 442376 | tf_op jit(solution)/shard_map/ppermute | solution.py:409
  127.4 19.0 %collective-permute-start.18 = (f32[4,72,128]{2,1,0:T(8,128)S(1)}, f32[4,72,128]{2,1,0:T(8,128)}, u32[]{:S(2)}, u32[]{:S(2)}) collective-permute-start(f32[4,72,128]{2,1,0:T(8,128)S(1)} %copy-done.11), channel_id=1, source_target_pairs={{0,80},{8,88},{16,96},{24,104},{32,112},{40,120},{48,0},{56,8},{64... | collective-permute-start | bytes 442376 | tf_op jit(solution)/shard_map/ppermute | solution.py:409
  128.1 18.3 %collective-permute-start.19 = (f32[4,72,128]{2,1,0:T(8,128)S(1)}, f32[4,72,128]{2,1,0:T(8,128)}, u32[]{:S(2)}, u32[]{:S(2)}) collective-permute-start(f32[4,72,128]{2,1,0:T(8,128)S(1)} %copy-done.9), channel_id=1, source_target_pairs={{0,112},{8,120},{16,0},{24,8},{32,16},{40,24},{48,32},{56,40},{64,... | collective-permute-start | bytes 442376 | tf_op jit(solution)/shard_map/ppermute | solution.py:409
  139.2 21.0 %all-to-all-start.2 = ((f32[8,1,2,144,128]{4,3,2,1,0:T(8,128)}), f32[8,1,2,144,128]{4,3,2,1,0:T(8,128)}, u32[]{:S(2)}, u32[]{:S(2)}) async-start(f32[8,1,2,144,128]{4,3,2,1,0:T(8,128)} %bitcast.12), calls=%async_computation.2 | async-start | bytes 2359296 | tf_op jit(solution)/shard_map/all_to_all | solution.py:401
  160.3 17.8 %all-to-all-start.3 = ((f32[8,1,2,144,128]{4,3,2,1,0:T(8,128)}), f32[8,1,2,144,128]{4,3,2,1,0:T(8,128)S(1)}, u32[]{:S(2)}, u32[]{:S(2)}) async-start(f32[8,1,2,144,128]{4,3,2,1,0:T(8,128)} %bitcast.13), calls=%async_computation.3 | async-start | bytes 2359296 | tf_op jit(solution)/shard_map/all_to_all | solution.py:401
  (24 other events, 352.5 us)

commit v2 on v1

--- a/solution.py
+++ b/solution.py
@@ -107,22 +107,22 @@
                 to_hi = pl.ds(lax.rem(place[0] + dh, 2), 1)
                 to_core = lax.rem(place[2] + dc, 2)
                 lanes = slice(0, LANES) if half == 0 else slice(LANES, ROWS)
-                for z in range(2):
+                for z in range(4):
                     store_lanes(outs[i].at[pl.ds(z, 1)], a[to_hi, z, to_core, 0, :, lanes], half)
             outs = outs[4:]
 
     parts = 8 * field
     shape = [jax.ShapeDtypeStruct((NZ, STRIP, LANES), jnp.float32)] * parts
-    spec = [pl.BlockSpec((2, STRIP, LANES), lambda i, place: (i, 0, 0))] * parts
+    spec = [pl.BlockSpec((4, STRIP, LANES), lambda i, place: (i, 0, 0))] * parts
     if field == 0:
         shape.insert(0, jax.ShapeDtypeStruct((2, NZ, 2, 2, STRIP, LANES), jnp.float32))
-        spec.insert(0, pl.BlockSpec((2, 2, 2, 2, STRIP, LANES), lambda i, place: (0, i, 0, 0, 0, 0)))
+        spec.insert(0, pl.BlockSpec((2, 4, 2, 2, STRIP, LANES), lambda i, place: (0, i, 0, 0, 0, 0)))
     return pl.pallas_call(
         kernel,
         grid_spec=pltpu.PrefetchScalarGridSpec(
             num_scalar_prefetch=1,
-            grid=(4,),
-            in_specs=[pl.BlockSpec((2, 2, 2, 1, STRIP, ROWS), lambda i, place: (0, i, 0, field, 0, 0))]
+            grid=(2,),
+            in_specs=[pl.BlockSpec((2, 4, 2, 1, STRIP, ROWS), lambda i, place: (0, i, 0, field, 0, 0))]
             + [pl.BlockSpec(memory_space=pl.ANY)] * len(after),
             out_specs=spec,
         ),
@@ -142,7 +142,7 @@
                 outs[dz - 1][i] = sources[i][to_z]
 
     shape = jax.ShapeDtypeStruct((4, STRIP, LANES), jnp.float32)
-    anywhere = pl.BlockSpec(memory_space=pl.ANY)
+    anywhere = pl.BlockSpec(memory_space=pltpu.HBM)
     local = pl.BlockSpec(memory_space=pltpu.VMEM)
     return pl.pallas_call(
         kernel,
@@ -206,7 +206,8 @@
     def kernel(place, *refs):
         sources = refs[: len(pieces)]
         table = refs[len(pieces)]
-        out, columns, folded, tables, sems, table_sem = refs[-6:]
+        result, out, columns, folded, tables, sems, table_sem, out_sem = refs[-8:]
+        stores = []
         load = pltpu.make_async_copy(table, tables, table_sem)
         copies = [[], []]
         if whole:
@@ -238,19 +239,25 @@
                 total = total.reshape(NJ, 2, 2, 8, LANES)
                 for group, number in enumerate((0, 9) if q == 0 else (q, 18 - q)):
                     out[:, half, :, number] = total[:, group]
-
-    anywhere = pl.BlockSpec(memory_space=pl.ANY)
+            stores.append(pltpu.make_async_copy(out.at[:, half], result.at[:, half], out_sem))
+            stores[half].start()
+        for store in stores:
+            store.wait()
+
+    anywhere = pl.BlockSpec(memory_space=pltpu.HBM)
     local = pl.BlockSpec(memory_space=pltpu.VMEM)
     shape = (NJ, halves, 2, 18, 8, LANES)
     return pl.pallas_call(
         kernel,
         in_specs=[pl.BlockSpec(memory_space=pltpu.SMEM)] + [anywhere] * (len(pieces) + 1 + len(after)),
-        out_specs=local,
+        out_specs=anywhere,
         scratch_shapes=[
+            pltpu.VMEM(shape, jnp.float32),
             pltpu.VMEM((halves, 32, STRIP, LANES), jnp.float32),
             pltpu.VMEM((NQ, 256, 256), jnp.bfloat16),
             pltpu.VMEM((NQ, 512, 256), jnp.bfloat16),
             pltpu.SemaphoreType.DMA((2,)),
+            pltpu.SemaphoreType.DMA,
             pltpu.SemaphoreType.DMA,
         ],
         out_shape=jax.ShapeDtypeStruct(shape, jnp.float32),
@@ -284,14 +291,16 @@
     return [add(e, o) for e, o in zip(even, odd)] + [sub(e, o) for e, o in zip(even, odd)]
 
 
-def y_kernel(count, *refs):
+def y_kernel(count, field, *refs):
     sources = refs[:count]
-    twiddle, main, weave = refs[count : count + 3]
-    out, gathered, high, low, mixed, woven, sems = refs[-7:]
+    twiddle, main_hbm, weave_hbm = refs[count : count + 3]
+    result, gathered, high, low, mixed, woven, main, weave, out, sems, out_sem = refs[-11:]
     copies = []
     for half in range(2):
         source = sources[0].at[:, half] if len(sources) == 1 else sources[half].at[:, 0]
         copies.append(pltpu.make_async_copy(source, gathered.at[half], sems.at[half]))
+    copies.append(pltpu.make_async_copy(main_hbm, main, sems.at[2]))
+    copies.append(pltpu.make_async_copy(weave_hbm, weave, sems.at[3]))
     for copy in copies:
         copy.start()
     for half in range(2):
@@ -316,6 +325,7 @@
 
         lax.fori_loop(0, 144 // TILE, fold, 0)
 
+    copies[2].wait()
     for c in range(NJ):
         a = high[c]
         value = (
@@ -330,7 +340,9 @@
             for group in range(18):
                 mixed[c, part, pl.ds(group, 8, stride=18), :] = piece[8 * group : 8 * group + 8]
 
+    copies[3].wait()
     slot = lax.broadcasted_iota(jnp.int32, (144, LANES), 1) // 32
+    stores = []
     for t in range(4):
         for comp in range(2):
             for upper in range(2):
@@ -351,25 +363,29 @@
                 tile = 4 * upper + t
                 width = min(256, NY - 256 * tile)
                 start = (2 * comp + upper) * 144
-                out[comp, 0, :, 256 * tile : 256 * tile + width] = product[start : start + 144, :width]
+                lanes = slice(256 * tile, 256 * tile + width)
+                out[comp, :, lanes] = product[start : start + 144, :width]
+                stores.append(pltpu.make_async_copy(out.at[comp, :, lanes], result.at[comp, field, :, lanes], out_sem))
+                stores[-1].start()
+    for store in stores:
+        store.wait()
 
 
 def y_transform(field, arrays, before):
     twiddle, main, weave = y_tables()
-    anywhere = pl.BlockSpec(memory_space=pl.ANY)
+    anywhere = pl.BlockSpec(memory_space=pltpu.HBM)
     local = pl.BlockSpec(memory_space=pltpu.VMEM)
     inputs = [*arrays, jnp.asarray(twiddle), jnp.asarray(main), jnp.asarray(weave)]
-    in_specs = [anywhere] * len(arrays) + [local] * 3
+    in_specs = [anywhere] * len(arrays) + [local] + [anywhere] * 2
     aliases = {}
     if before is not None:
         aliases = {len(inputs): 0}
         inputs.append(before)
         in_specs.append(anywhere)
     return pl.pallas_call(
-        functools.partial(y_kernel, len(arrays)),
-        grid=(1,),
+        functools.partial(y_kernel, len(arrays), field),
         in_specs=in_specs,
-        out_specs=pl.BlockSpec((2, 1, 144, NY), lambda i: (0, field, 0, 0)),
+        out_specs=anywhere,
         out_shape=jax.ShapeDtypeStruct((2, 2, 144, NY), jnp.float32),
         scratch_shapes=[
             pltpu.VMEM((2, NJ, 2, 144, LANES), jnp.float32),
@@ -377,7 +393,11 @@
             pltpu.VMEM((NJ, 144, 512), jnp.bfloat16),
             pltpu.VMEM((NJ, 4, 144, LANES), jnp.float32),
             pltpu.VMEM((1152, 256), jnp.bfloat16),
-            pltpu.SemaphoreType.DMA((2,)),
+            pltpu.VMEM((2, 512, 512), jnp.bfloat16),
+            pltpu.VMEM((4, 256, 256), jnp.bfloat16),
+            pltpu.VMEM((2, 144, NY), jnp.float32),
+            pltpu.SemaphoreType.DMA((4,)),
+            pltpu.SemaphoreType.DMA,
         ],
         input_output_aliases=aliases,
         compiler_params=compiler_params(),
@@ -425,10 +445,11 @@
     sends = [list(pack_z(place, part, [])) for part in parts]
     second = over_z(sends[0], (1, 7, 2, 6))
     first, sends, second = lax.optimization_barrier((first, sends, second))
+    flying = over_z(sends[0], (4,))
     x01 = x_transform(place, [first], [], 2 * 10**10)
-    x01, sends = lax.optimization_barrier((x01, sends))
+    x01, sends, flying = lax.optimization_barrier((x01, sends, flying))
     g01 = over_y(x01)
-    second |= over_z(sends[0], (4, 3, 5))
+    second |= flying | over_z(sends[0], (3, 5))
     flying = over_z(sends[1], (4, 2, 6))
     third = over_z(sends[1], (3, 5, 1, 7))
     x2 = x_transform(place, parts[0] + listed(second), [], 2 * 10**10)

time: 188 us -> 178 us (0.947)
  starting transfers between devices: 71.5 us -> 62.5 us
  Pallas kernels: 49.5 us -> 45 us
  waiting for transfers between devices: 60.9 us -> 63.5 us
    ppermute x14, starting transfers between devices: 36.2 us -> 30.2 us  [over_z(): lax.ppermute(sends[dz - 1], 'gx', shift(0, dz, 0))]
    all_to_all x3, starting transfers between devices: 17.9 us -> 14.8 us  [over_y(): return lax.all_to_all(blocks, 'gy', split_axis=0, concat_axis=0, tiled=True)]
    pallas_call x2, Pallas kernels: 9.31 us -> 6.94 us  [pack(): pl.pallas_call(kernel, grid_spec=pltpu.PrefetchScalarGridSpec(num_scalar_...]
  transfers between devices with their start and end apart: 24 -> 24, of which waited for: 11 -> 11; matrix products, arithmetic and copies ran while one was open for 0% -> 0% of each run, Pallas kernels for 15% -> 19%
where the time goes in v2:
time: 178 us; the launch traced here: 176 us
  waiting for transfers between devices  63.5 us (36%)
  starting transfers between devices  62.5 us (35%)
  Pallas kernels  45 us (25%)
  local copies, waits for them, and re-layouts  3.81 us (2%)
    ppermute x6, waiting for transfers between devices, over_xh(): lax.ppermute(part, 'gx', shift(dh, 0, dc))  33.2 us
    ppermute x14, starting transfers between devices, over_z(): lax.ppermute(sends[dz - 1], 'gx', shift(0, dz, 0))  30.2 us
    pallas_call x3, Pallas kernels, x_transform(): pl.pallas_call(kernel, in_specs=[pl.BlockSpec(memory_space=pltpu.SMEM)] +...  18.7 us
    ppermute x14, waiting for transfers between devices, over_z(): lax.ppermute(sends[dz - 1], 'gx', shift(0, dz, 0))  17.1 us
    all_to_all x3, starting transfers between devices, over_y(): return lax.all_to_all(blocks, 'gy', split_axis=0, concat_axis=0, tiled=True)  14.8 us
    pallas_call x2, Pallas kernels, y_transform(): pl.pallas_call(functools.partial(y_kernel, len(arrays), field), in_specs=...  14.7 us
    all_to_all x3, waiting for transfers between devices, over_y(): return lax.all_to_all(blocks, 'gy', split_axis=0, concat_axis=0, tiled=True)  13.3 us
    all_to_all x1, starting transfers between devices, body(): first = lax.all_to_all(first, 'gx', split_axis=0, concat_axis=0, tiled=True)  10.7 us
  transfers between devices with their start and end apart: 24, of which 11 were waited for; matrix products, arithmetic and copies ran while one was open for 0% of the time, Pallas kernels for 19%

profile of v2, /device:TPU:68, one launch (start us, length us, event | category | flops | bytes accessed | tf_op | source)
XLA Modules:
  0.0 175.9 jit_solution(839962177538040423)
XLA Ops:
  0.6 3.5 %pack.2.refs_0_ = f32[2,8,2,2,72,128]{5,4,3,2,1,0:T(8,128)} custom-call(s32[3]{0:T(128)} %pad_add_fusion.place, f32[2,8,2,2,72,250]{5,4,3,2,1,0:T(8,128)} %bitcast.9), custom_call_target="tpu_custom_call" | custom-call | tf_op jit(solution)/shard_map/pack/pallas_call | solution.py:120
  4.1 10.7 %all-to-all-start = ((f32[32,2,72,128]{3,2,1,0:T(8,128)}), f32[32,2,72,128]{3,2,1,0:T(8,128)S(1)}, u32[]{:S(2)}, u32[]{:S(2)}) async-start(f32[32,2,72,128]{3,2,1,0:T(8,128)} %bitcast.8), calls=%async_computation | async-start | bytes 4718592 | tf_op jit(solution)/shard_map/all_to_all | solution.py:443
  14.8 3.5 %pack.3 = (f32[8,72,128]{2,1,0:T(8,128)}, f32[8,72,128]{2,1,0:T(8,128)}, f32[8,72,128]{2,1,0:T(8,128)}, f32[8,72,128]{2,1,0:T(8,128)}, f32[8,72,128]{2,1,0:T(8,1...) custom-call(s32[3]{0:T(128)} %pad_add_fusion.place, f32[2,8,2,2,72,250]{5,4,3,2,1,0:T(8,128)} %bitcast.10, ...), custom_call_target="tpu_custom_call" | custom-call | tf_op jit(solution)/shard_map/pack/pallas_call | solution.py:120
  25.1 10.0 %collective-permute-done.1.refs_2_ = f32[8,72,128]{2,1,0:T(8,128)S(1)} collective-permute-done((f32[8,72,128]{2,1,0:T(8,128)}, f32[8,72,128]{2,1,0:T(8,128)S(1)}, u32[]{:S(2)}, u32[]{:S(2)}) %collective-permute-start.1) | collective-permute-done | bytes 294944 | tf_op jit(solution)/shard_map/ppermute | solution.py:425
  35.1 12.3 %collective-permute-done.2.refs_3_ = f32[8,72,128]{2,1,0:T(8,128)} collective-permute-done((f32[8,72,128]{2,1,0:T(8,128)}, f32[8,72,128]{2,1,0:T(8,128)}, u32[]{:S(2)}, u32[]{:S(2)}) %collective-permute-start.2) | collective-permute-done | bytes 294944 | tf_op jit(solution)/shard_map/ppermute | solution.py:425
  51.5 3.2 %collective-permute-start.7 = (f32[4,72,128]{2,1,0:T(8,128)}, f32[4,72,128]{2,1,0:T(8,128)S(1)}, u32[]{:S(2)}, u32[]{:S(2)}) collective-permute-start(f32[4,72,128]{2,1,0:T(8,128)} %get-tuple-element.66), channel_id=1, source_target_pairs={{0,32},{8,40},{16,48},{24,56},{32,64},{40,72},{48,80},{56,88},{64,... | collective-permute-start | bytes 442376 | tf_op jit(solution)/shard_map/ppermute | solution.py:429
  54.8 4.0 %collective-permute-done.4.refs_2_ = f32[8,72,128]{2,1,0:T(8,128)S(1)} collective-permute-done((f32[8,72,128]{2,1,0:T(8,128)}, f32[8,72,128]{2,1,0:T(8,128)S(1)}, u32[]{:S(2)}, u32[]{:S(2)}) %collective-permute-start.4) | collective-permute-done | bytes 294944 | tf_op jit(solution)/shard_map/ppermute | solution.py:425
  61.1 6.8 %collective-permute-done.5.refs_3_ = f32[8,72,128]{2,1,0:T(8,128)S(1)} collective-permute-done((f32[8,72,128]{2,1,0:T(8,128)}, f32[8,72,128]{2,1,0:T(8,128)S(1)}, u32[]{:S(2)}, u32[]{:S(2)}) %collective-permute-start.5) | collective-permute-done | bytes 294944 | tf_op jit(solution)/shard_map/ppermute | solution.py:425
  70.9 4.4 %collective-permute-done.7.refs_5_ = f32[4,72,128]{2,1,0:T(8,128)S(1)} collective-permute-done((f32[4,72,128]{2,1,0:T(8,128)}, f32[4,72,128]{2,1,0:T(8,128)S(1)}, u32[]{:S(2)}, u32[]{:S(2)}) %collective-permute-start.7) | collective-permute-done | bytes 147488 | tf_op jit(solution)/shard_map/ppermute | solution.py:429
  77.5 5.2 %collective-permute-start.10 = (f32[4,72,128]{2,1,0:T(8,128)}, f32[4,72,128]{2,1,0:T(8,128)S(1)}, u32[]{:S(2)}, u32[]{:S(2)}) collective-permute-start(f32[4,72,128]{2,1,0:T(8,128)} %get-tuple-element.85), channel_id=1, source_target_pairs={{0,64},{8,72},{16,80},{24,88},{32,96},{40,104},{48,112},{56,120},{... | collective-permute-start | bytes 442376 | tf_op jit(solution)/shard_map/ppermute | solution.py:429
  82.7 8.0 %x_transform.3 = f32[8,2,2,18,8,128]{5,4,3,2,1,0:T(8,128)} custom-call(s32[3]{0:T(128)} %pad_add_fusion.place, f32[32,2,72,128]{3,2,1,0:T(8,128)} %copy-done.2, bf16[9,512,256]{2,1,0:T(8,128)(2,1)} %constant.59.clone.refs_1_.refs_11_), custom_call_target="tpu_custom_call" | custom-call | flops 20000000000 | tf_op jit(solution)/shard_map/x_transform/pallas_call | solution.py:250
  91.4 5.2 %all-to-all-start.1 = ((f32[8,2,2,144,128]{4,3,2,1,0:T(8,128)}), f32[8,2,2,144,128]{4,3,2,1,0:T(8,128)S(1)}, u32[]{:S(2)}, u32[]{:S(2)}) async-start(f32[8,2,2,144,128]{4,3,2,1,0:T(8,128)} %bitcast.11), calls=%async_computation.1 | async-start | bytes 4718592 | tf_op jit(solution)/shard_map/all_to_all | solution.py:421
  96.7 4.2 %collective-permute-start.11 = (f32[4,72,128]{2,1,0:T(8,128)S(1)}, f32[4,72,128]{2,1,0:T(8,128)S(1)}, u32[]{:S(2)}, u32[]{:S(2)}) collective-permute-start(f32[4,72,128]{2,1,0:T(8,128)S(1)} %copy-done.17), channel_id=1, source_target_pairs={{0,48},{8,56},{16,64},{24,72},{32,80},{40,88},{48,96},{56,104},{64... | collective-permute-start | bytes 442376 | tf_op jit(solution)/shard_map/ppermute | solution.py:429
  110.9 5.0 %collective-permute-done.12.refs_8_ = f32[4,72,128]{2,1,0:T(8,128)S(1)} collective-permute-done((f32[4,72,128]{2,1,0:T(8,128)S(1)}, f32[4,72,128]{2,1,0:T(8,128)S(1)}, u32[]{:S(2)}, u32[]{:S(2)}) %collective-permute-start.12) | collective-permute-done | bytes 147488 | tf_op jit(solution)/shard_map/ppermute | solution.py:429
  117.0 4.0 %collective-permute-start.18 = (f32[4,72,128]{2,1,0:T(8,128)S(1)}, f32[4,72,128]{2,1,0:T(8,128)}, u32[]{:S(2)}, u32[]{:S(2)}) collective-permute-start(f32[4,72,128]{2,1,0:T(8,128)S(1)} %copy-done.11), channel_id=1, source_target_pairs={{0,80},{8,88},{16,96},{24,104},{32,112},{40,120},{48,0},{56,8},{64... | collective-permute-start | bytes 442376 | tf_op jit(solution)/shard_map/ppermute | solution.py:429
  121.0 4.6 %collective-permute-done.14.refs_7_ = f32[4,72,128]{2,1,0:T(8,128)} collective-permute-done((f32[4,72,128]{2,1,0:T(8,128)}, f32[4,72,128]{2,1,0:T(8,128)}, u32[]{:S(2)}, u32[]{:S(2)}) %collective-permute-start.14) | collective-permute-done | bytes 147488 | tf_op jit(solution)/shard_map/ppermute | solution.py:429
  125.6 5.4 %x_transform.4.refs_12_ = f32[8,1,2,18,8,128]{5,4,3,2,1,0:T(8,128)} custom-call(s32[3]{0:T(128)} %pad_add_fusion.place, f32[8,72,128]{2,1,0:T(8,128)} %get-tuple-element.61.refs_0_, f32[8,72,128]{2,1,0:T(8,128)} %copy-done.6, f32[8,72,128]{2,1,0:T(8,128)} %copy-done.7, f32[8,72,128]{2,1,0:T(8,128)} %collective-permute-done.2.refs_3_, ...), custom_call_target="tpu_custom_call" | custom-call | flops 20000000000 | tf_op jit(solution)/shard_map/x_transform/pallas_call | solution.py:250
  131.0 5.8 %all-to-all-start.2 = ((f32[8,1,2,144,128]{4,3,2,1,0:T(8,128)}), f32[8,1,2,144,128]{4,3,2,1,0:T(8,128)}, u32[]{:S(2)}, u32[]{:S(2)}) async-start(f32[8,1,2,144,128]{4,3,2,1,0:T(8,128)} %bitcast.12), calls=%async_computation.2 | async-start | bytes 2359296 | tf_op jit(solution)/shard_map/all_to_all | solution.py:421
  137.5 5.4 %x_transform.5 = f32[8,1,2,18,8,128]{5,4,3,2,1,0:T(8,128)} custom-call(s32[3]{0:T(128)} %pad_add_fusion.place, f32[8,72,128]{2,1,0:T(8,128)} %get-tuple-element.72.refs_0_, f32[8,72,128]{2,1,0:T(8,128)} %copy-done.3, f32[8,72,128]{2,1,0:T(8,128)} %copy-done.4, f32[8,72,128]{2,1,0:T(8,128)} %copy-done.5, f32[4,72,128]{2,1,0:T(8,128)} %copy-done.19, ...), custom_call_target="tpu_custom_call" | custom-call | flops 199999995904 | tf_op jit(solution)/shard_map/x_transform/pallas_call | solution.py:250
  142.8 7.8 %all-to-all-done.2.refs_0_ = f32[8,1,2,144,128]{4,3,2,1,0:T(8,128)} async-done(((f32[8,1,2,144,128]{4,3,2,1,0:T(8,128)}), f32[8,1,2,144,128]{4,3,2,1,0:T(8,128)}, u32[]{:S(2)}, u32[]{:S(2)}) %all-to-all-start.2) | async-done | bytes 1179680 | tf_op jit(solution)/shard_map/all_to_all | solution.py:421
  150.6 3.8 %all-to-all-start.3 = ((f32[8,1,2,144,128]{4,3,2,1,0:T(8,128)}), f32[8,1,2,144,128]{4,3,2,1,0:T(8,128)S(1)}, u32[]{:S(2)}, u32[]{:S(2)}) async-start(f32[8,1,2,144,128]{4,3,2,1,0:T(8,128)} %bitcast.13), calls=%async_computation.3 | async-start | bytes 2359296 | tf_op jit(solution)/shard_map/all_to_all | solution.py:421
  154.4 7.4 %y_transform.2.refs_5_ = f32[2,2,144,2000]{3,2,1,0:T(8,128)} custom-call(f32[8,2,2,144,128]{4,3,2,1,0:T(8,128)} %copy-done, f32[2,8,2,128]{3,2,1,0:T(2,128)} %constant.60.clone.refs_1_.refs_2_, bf16[2,512,512]{2,1,0:T(8,128)(2,1)} %constant.61.clone.refs_2_.refs_3_, bf16[4,256,256]{2,1,0:T(8,128)(2,1)} %constant.62.clone.refs_3_.refs_4_), custom_call_target="tpu_custom_call" | custom-call | tf_op jit(solution)/shard_map/y_transform/pallas_call | solution.py:385
  161.8 5.5 %all-to-all-done.3.refs_1_ = f32[8,1,2,144,128]{4,3,2,1,0:T(8,128)S(1)} async-done(((f32[8,1,2,144,128]{4,3,2,1,0:T(8,128)}), f32[8,1,2,144,128]{4,3,2,1,0:T(8,128)S(1)}, u32[]{:S(2)}, u32[]{:S(2)}) %all-to-all-start.3) | async-done | bytes 1179680 | tf_op jit(solution)/shard_map/all_to_all | solution.py:421
  168.4 7.4 %y_transform.3 = f32[2,2,144,2000]{3,2,1,0:T(8,128)} custom-call(f32[8,1,2,144,128]{4,3,2,1,0:T(8,128)} %all-to-all-done.2.refs_0_, f32[8,1,2,144,128]{4,3,2,1,0:T(8,128)} %copy-done.1, f32[2,8,2,128]{3,2,1,0:T(2,128)} %constant.60.clone.refs_1_.refs_2_, bf16[2,512,512]{2,1,0:T(8,128)(2,1)} %constant.61.clone.refs_2_.refs_3_, ...), custom_call_target="tpu_custom_call", output_to_operand_aliasing={{}: (5, {})} | custom-call | tf_op jit(solution)/shard_map/y_transform/pallas_call | solution.py:385
  (82 shorter events, 32.6 us)
Async XLA Ops:
  4.1 73.4 %all-to-all-start = ((f32[32,2,72,128]{3,2,1,0:T(8,128)}), f32[32,2,72,128]{3,2,1,0:T(8,128)S(1)}, u32[]{:S(2)}, u32[]{:S(2)}) async-start(f32[32,2,72,128]{3,2,1,0:T(8,128)} %bitcast.8), calls=%async_computation | async-start | bytes 4718592 | tf_op jit(solution)/shard_map/all_to_all | solution.py:443
  18.3 4.4 %collective-permute-start = (f32[8,72,128]{2,1,0:T(8,128)}, f32[8,72,128]{2,1,0:T(8,128)S(1)}, u32[]{:S(2)}, u32[]{:S(2)}) collective-permute-start(f32[8,72,128]{2,1,0:T(8,128)} %get-tuple-element.62), channel_id=1, source_target_pairs={{0,8},{8,0},{16,24},{24,16},{32,40},{40,32},{48,56},{56,48},{64,72... | collective-permute-start | bytes 884744 | tf_op jit(solution)/shard_map/ppermute | solution.py:425
  18.5 16.6 %collective-permute-start.1 = (f32[8,72,128]{2,1,0:T(8,128)}, f32[8,72,128]{2,1,0:T(8,128)S(1)}, u32[]{:S(2)}, u32[]{:S(2)}) collective-permute-start(f32[8,72,128]{2,1,0:T(8,128)} %get-tuple-element.63), channel_id=1, source_target_pairs={{0,128},{8,136},{16,144},{24,152},{32,160},{40,168},{48,176},{56,1... | collective-permute-start | bytes 884744 | tf_op jit(solution)/shard_map/ppermute | solution.py:425
  19.1 28.4 %collective-permute-start.2 = (f32[8,72,128]{2,1,0:T(8,128)}, f32[8,72,128]{2,1,0:T(8,128)}, u32[]{:S(2)}, u32[]{:S(2)}) collective-permute-start(f32[8,72,128]{2,1,0:T(8,128)} %get-tuple-element.64), channel_id=1, source_target_pairs={{0,136},{8,128},{16,152},{24,144},{32,168},{40,160},{48,184},{56,1... | collective-permute-start | bytes 884744 | tf_op jit(solution)/shard_map/ppermute | solution.py:425
  21.7 33.0 %collective-permute-start.3 = (f32[8,72,128]{2,1,0:T(8,128)}, f32[8,72,128]{2,1,0:T(8,128)S(1)}, u32[]{:S(2)}, u32[]{:S(2)}) collective-permute-start(f32[8,72,128]{2,1,0:T(8,128)} %get-tuple-element.73), channel_id=1, source_target_pairs={{0,8},{8,0},{16,24},{24,16},{32,40},{40,32},{48,56},{56,48},{64,72... | collective-permute-start | bytes 884744 | tf_op jit(solution)/shard_map/ppermute | solution.py:425
  22.2 36.6 %collective-permute-start.4 = (f32[8,72,128]{2,1,0:T(8,128)}, f32[8,72,128]{2,1,0:T(8,128)S(1)}, u32[]{:S(2)}, u32[]{:S(2)}) collective-permute-start(f32[8,72,128]{2,1,0:T(8,128)} %get-tuple-element.74), channel_id=1, source_target_pairs={{0,128},{8,136},{16,144},{24,152},{32,160},{40,168},{48,176},{56,1... | collective-permute-start | bytes 884744 | tf_op jit(solution)/shard_map/ppermute | solution.py:425
  22.7 45.2 %collective-permute-start.5 = (f32[8,72,128]{2,1,0:T(8,128)}, f32[8,72,128]{2,1,0:T(8,128)S(1)}, u32[]{:S(2)}, u32[]{:S(2)}) collective-permute-start(f32[8,72,128]{2,1,0:T(8,128)} %get-tuple-element.75), channel_id=1, source_target_pairs={{0,136},{8,128},{16,152},{24,144},{32,168},{40,160},{48,184},{56,1... | collective-permute-start | bytes 884744 | tf_op jit(solution)/shard_map/ppermute | solution.py:425
  49.8 21.1 %collective-permute-start.6 = (f32[4,72,128]{2,1,0:T(8,128)}, f32[4,72,128]{2,1,0:T(8,128)S(1)}, u32[]{:S(2)}, u32[]{:S(2)}) collective-permute-start(f32[4,72,128]{2,1,0:T(8,128)} %get-tuple-element.65), channel_id=1, source_target_pairs={{0,16},{8,24},{16,32},{24,40},{32,48},{40,56},{48,64},{56,72},{64,... | collective-permute-start | bytes 442376 | tf_op jit(solution)/shard_map/ppermute | solution.py:429
  51.5 23.8 %collective-permute-start.7 = (f32[4,72,128]{2,1,0:T(8,128)}, f32[4,72,128]{2,1,0:T(8,128)S(1)}, u32[]{:S(2)}, u32[]{:S(2)}) collective-permute-start(f32[4,72,128]{2,1,0:T(8,128)} %get-tuple-element.66), channel_id=1, source_target_pairs={{0,32},{8,40},{16,48},{24,56},{32,64},{40,72},{48,80},{56,88},{64,... | collective-permute-start | bytes 442376 | tf_op jit(solution)/shard_map/ppermute | solution.py:429
  54.8 22.1 %collective-permute-start.8 = (f32[4,72,128]{2,1,0:T(8,128)}, f32[4,72,128]{2,1,0:T(8,128)S(1)}, u32[]{:S(2)}, u32[]{:S(2)}) collective-permute-start(f32[4,72,128]{2,1,0:T(8,128)} %get-tuple-element.70), channel_id=1, source_target_pairs={{0,96},{8,104},{16,112},{24,120},{32,0},{40,8},{48,16},{56,24},{64... | collective-permute-start | bytes 442376 | tf_op jit(solution)/shard_map/ppermute | solution.py:429
  58.8 18.7 %collective-permute-start.9 = (f32[4,72,128]{2,1,0:T(8,128)}, f32[4,72,128]{2,1,0:T(8,128)}, u32[]{:S(2)}, u32[]{:S(2)}) collective-permute-start(f32[4,72,128]{2,1,0:T(8,128)} %get-tuple-element.71), channel_id=1, source_target_pairs={{0,112},{8,120},{16,0},{24,8},{32,16},{40,24},{48,32},{56,40},{64,... | collective-permute-start | bytes 442376 | tf_op jit(solution)/shard_map/ppermute | solution.py:429
  77.5 13.2 %collective-permute-start.10 = (f32[4,72,128]{2,1,0:T(8,128)}, f32[4,72,128]{2,1,0:T(8,128)S(1)}, u32[]{:S(2)}, u32[]{:S(2)}) collective-permute-start(f32[4,72,128]{2,1,0:T(8,128)} %get-tuple-element.85), channel_id=1, source_target_pairs={{0,64},{8,72},{16,80},{24,88},{32,96},{40,104},{48,112},{56,120},{... | collective-permute-start | bytes 442376 | tf_op jit(solution)/shard_map/ppermute | solution.py:429
  91.4 39.5 %all-to-all-start.1 = ((f32[8,2,2,144,128]{4,3,2,1,0:T(8,128)}), f32[8,2,2,144,128]{4,3,2,1,0:T(8,128)S(1)}, u32[]{:S(2)}, u32[]{:S(2)}) async-start(f32[8,2,2,144,128]{4,3,2,1,0:T(8,128)} %bitcast.11), calls=%async_computation.1 | async-start | bytes 4718592 | tf_op jit(solution)/shard_map/all_to_all | solution.py:421
  96.7 13.0 %collective-permute-start.11 = (f32[4,72,128]{2,1,0:T(8,128)S(1)}, f32[4,72,128]{2,1,0:T(8,128)S(1)}, u32[]{:S(2)}, u32[]{:S(2)}) collective-permute-start(f32[4,72,128]{2,1,0:T(8,128)S(1)} %copy-done.17), channel_id=1, source_target_pairs={{0,48},{8,56},{16,64},{24,72},{32,80},{40,88},{48,96},{56,104},{64... | collective-permute-start | bytes 442376 | tf_op jit(solution)/shard_map/ppermute | solution.py:429
  100.9 15.0 %collective-permute-start.12 = (f32[4,72,128]{2,1,0:T(8,128)S(1)}, f32[4,72,128]{2,1,0:T(8,128)S(1)}, u32[]{:S(2)}, u32[]{:S(2)}) collective-permute-start(f32[4,72,128]{2,1,0:T(8,128)S(1)} %copy-done.16), channel_id=1, source_target_pairs={{0,80},{8,88},{16,96},{24,104},{32,112},{40,120},{48,0},{56,8},{64... | collective-permute-start | bytes 442376 | tf_op jit(solution)/shard_map/ppermute | solution.py:429
  101.8 15.2 %collective-permute-start.13 = (f32[4,72,128]{2,1,0:T(8,128)}, f32[4,72,128]{2,1,0:T(8,128)S(1)}, u32[]{:S(2)}, u32[]{:S(2)}) collective-permute-start(f32[4,72,128]{2,1,0:T(8,128)} %get-tuple-element.102), channel_id=1, source_target_pairs={{0,32},{8,40},{16,48},{24,56},{32,64},{40,72},{48,80},{56,88},{64,... | collective-permute-start | bytes 442376 | tf_op jit(solution)/shard_map/ppermute | solution.py:429
  103.4 22.2 %collective-permute-start.14 = (f32[4,72,128]{2,1,0:T(8,128)}, f32[4,72,128]{2,1,0:T(8,128)}, u32[]{:S(2)}, u32[]{:S(2)}) collective-permute-start(f32[4,72,128]{2,1,0:T(8,128)} %get-tuple-element.103), channel_id=1, source_target_pairs={{0,64},{8,72},{16,80},{24,88},{32,96},{40,104},{48,112},{56,120},{... | collective-permute-start | bytes 442376 | tf_op jit(solution)/shard_map/ppermute | solution.py:429
  106.0 24.9 %collective-permute-start.15 = (f32[4,72,128]{2,1,0:T(8,128)S(1)}, f32[4,72,128]{2,1,0:T(8,128)}, u32[]{:S(2)}, u32[]{:S(2)}) collective-permute-start(f32[4,72,128]{2,1,0:T(8,128)S(1)} %copy-done.15), channel_id=1, source_target_pairs={{0,96},{8,104},{16,112},{24,120},{32,0},{40,8},{48,16},{56,24},{64... | collective-permute-start | bytes 442376 | tf_op jit(solution)/shard_map/ppermute | solution.py:429
  109.7 27.1 %collective-permute-start.16 = (f32[4,72,128]{2,1,0:T(8,128)S(1)}, f32[4,72,128]{2,1,0:T(8,128)S(1)}, u32[]{:S(2)}, u32[]{:S(2)}) collective-permute-start(f32[4,72,128]{2,1,0:T(8,128)S(1)} %copy-done.13), channel_id=1, source_target_pairs={{0,16},{8,24},{16,32},{24,40},{32,48},{40,56},{48,64},{56,72},{64,... | collective-permute-start | bytes 442376 | tf_op jit(solution)/shard_map/ppermute | solution.py:429
  115.9 20.9 %collective-permute-start.17 = (f32[4,72,128]{2,1,0:T(8,128)S(1)}, f32[4,72,128]{2,1,0:T(8,128)S(1)}, u32[]{:S(2)}, u32[]{:S(2)}) collective-permute-start(f32[4,72,128]{2,1,0:T(8,128)S(1)} %copy-done.12), channel_id=1, source_target_pairs={{0,48},{8,56},{16,64},{24,72},{32,80},{40,88},{48,96},{56,104},{64... | collective-permute-start | bytes 442376 | tf_op jit(solution)/shard_map/ppermute | solution.py:429
  117.0 19.8 %collective-permute-start.18 = (f32[4,72,128]{2,1,0:T(8,128)S(1)}, f32[4,72,128]{2,1,0:T(8,128)}, u32[]{:S(2)}, u32[]{:S(2)}) collective-permute-start(f32[4,72,128]{2,1,0:T(8,128)S(1)} %copy-done.11), channel_id=1, source_target_pairs={{0,80},{8,88},{16,96},{24,104},{32,112},{40,120},{48,0},{56,8},{64... | collective-permute-start | bytes 442376 | tf_op jit(solution)/shard_map/ppermute | solution.py:429
  125.5 11.3 %collective-permute-start.19 = (f32[4,72,128]{2,1,0:T(8,128)S(1)}, f32[4,72,128]{2,1,0:T(8,128)}, u32[]{:S(2)}, u32[]{:S(2)}) collective-permute-start(f32[4,72,128]{2,1,0:T(8,128)S(1)} %copy-done.9), channel_id=1, source_target_pairs={{0,112},{8,120},{16,0},{24,8},{32,16},{40,24},{48,32},{56,40},{64,... | collective-permute-start | bytes 442376 | tf_op jit(solution)/shard_map/ppermute | solution.py:429
  131.0 19.7 %all-to-all-start.2 = ((f32[8,1,2,144,128]{4,3,2,1,0:T(8,128)}), f32[8,1,2,144,128]{4,3,2,1,0:T(8,128)}, u32[]{:S(2)}, u32[]{:S(2)}) async-start(f32[8,1,2,144,128]{4,3,2,1,0:T(8,128)} %bitcast.12), calls=%async_computation.2 | async-start | bytes 2359296 | tf_op jit(solution)/shard_map/all_to_all | solution.py:421
  150.6 16.7 %all-to-all-start.3 = ((f32[8,1,2,144,128]{4,3,2,1,0:T(8,128)}), f32[8,1,2,144,128]{4,3,2,1,0:T(8,128)S(1)}, u32[]{:S(2)}, u32[]{:S(2)}) async-start(f32[8,1,2,144,128]{4,3,2,1,0:T(8,128)} %bitcast.13), calls=%async_computation.3 | async-start | bytes 2359296 | tf_op jit(solution)/shard_map/all_to_all | solution.py:421
  (24 other events, 287.3 us)

commit v3 on v2

--- a/solution.py
+++ b/solution.py
@@ -437,7 +437,7 @@
     me = lax.axis_index("gx")
     place = jnp.stack([me // 16, me // 2 % NZ, me % 2]).astype(jnp.int32)
     fields = fields.reshape(2, NZ, 2, 2, STRIP, ROWS)
-    first = pack(place, fields, 0, [])[0]
+    first = pack(jnp.zeros(3, jnp.int32), fields, 0, [])[0]
     rest = list(pack(place, fields, 1, [first]))
     first = first.reshape(32, 2, STRIP, LANES)
     first = lax.all_to_all(first, "gx", split_axis=0, concat_axis=0, tiled=True)

time: 178 us -> 178 us (level)
  no operation moved by 1% of the time
where the time goes in v3:
time: 178 us; the launch traced here: 176 us
  starting transfers between devices  63.1 us (35%)
  waiting for transfers between devices  62.3 us (35%)
  Pallas kernels  45 us (25%)
  local copies, waits for them, and re-layouts  4.38 us (2%)
    ppermute x6, waiting for transfers between devices, over_xh(): lax.ppermute(part, 'gx', shift(dh, 0, dc))  32.2 us
    ppermute x14, starting transfers between devices, over_z(): lax.ppermute(sends[dz - 1], 'gx', shift(0, dz, 0))  30.8 us
    pallas_call x3, Pallas kernels, x_transform(): pl.pallas_call(kernel, in_specs=[pl.BlockSpec(memory_space=pltpu.SMEM)] +...  18.7 us
    ppermute x14, waiting for transfers between devices, over_z(): lax.ppermute(sends[dz - 1], 'gx', shift(0, dz, 0))  16.8 us
    all_to_all x3, starting transfers between devices, over_y(): return lax.all_to_all(blocks, 'gy', split_axis=0, concat_axis=0, tiled=True)  14.8 us
    pallas_call x2, Pallas kernels, y_transform(): pl.pallas_call(functools.partial(y_kernel, len(arrays), field), in_specs=...  14.7 us
    all_to_all x3, waiting for transfers between devices, over_y(): return lax.all_to_all(blocks, 'gy', split_axis=0, concat_axis=0, tiled=True)  13.3 us
    all_to_all x1, starting transfers between devices, body(): first = lax.all_to_all(first, 'gx', split_axis=0, concat_axis=0, tiled=True)  10.7 us
  transfers between devices with their start and end apart: 24, of which 11 were waited for; matrix products, arithmetic and copies ran while one was open for 0% of the time, Pallas kernels for 19%

profile of v3, /device:TPU:68, one launch (start us, length us, event | category | flops | bytes accessed | tf_op | source)
XLA Modules:
  0.0 175.9 jit_solution(16932725334968327635)
XLA Ops:
  0.6 3.5 %pack.2.refs_0_ = f32[2,8,2,2,72,128]{5,4,3,2,1,0:T(8,128)} custom-call(s32[3]{0:T(128)} %broadcast_1_place.2.place, f32[2,8,2,2,72,250]{5,4,3,2,1,0:T(8,128)} %bitcast.9), custom_call_target="tpu_custom_call" | custom-call | tf_op jit(solution)/shard_map/pack/pallas_call | solution.py:120
  4.0 10.7 %all-to-all-start = ((f32[32,2,72,128]{3,2,1,0:T(8,128)}), f32[32,2,72,128]{3,2,1,0:T(8,128)S(1)}, u32[]{:S(2)}, u32[]{:S(2)}) async-start(f32[32,2,72,128]{3,2,1,0:T(8,128)} %bitcast.8), calls=%async_computation | async-start | bytes 4718592 | tf_op jit(solution)/shard_map/all_to_all | solution.py:443
  15.4 3.5 %pack.3 = (f32[8,72,128]{2,1,0:T(8,128)}, f32[8,72,128]{2,1,0:T(8,128)}, f32[8,72,128]{2,1,0:T(8,128)}, f32[8,72,128]{2,1,0:T(8,128)}, f32[8,72,128]{2,1,0:T(8,1...) custom-call(s32[3]{0:T(128)} %pad_add_fusion.place, f32[2,8,2,2,72,250]{5,4,3,2,1,0:T(8,128)} %bitcast.10, ...), custom_call_target="tpu_custom_call" | custom-call | tf_op jit(solution)/shard_map/pack/pallas_call | solution.py:120
  25.7 9.6 %collective-permute-done.1.refs_2_ = f32[8,72,128]{2,1,0:T(8,128)S(1)} collective-permute-done((f32[8,72,128]{2,1,0:T(8,128)}, f32[8,72,128]{2,1,0:T(8,128)S(1)}, u32[]{:S(2)}, u32[]{:S(2)}) %collective-permute-start.1) | collective-permute-done | bytes 294944 | tf_op jit(solution)/shard_map/ppermute | solution.py:425
  35.3 12.3 %collective-permute-done.2.refs_3_ = f32[8,72,128]{2,1,0:T(8,128)} collective-permute-done((f32[8,72,128]{2,1,0:T(8,128)}, f32[8,72,128]{2,1,0:T(8,128)}, u32[]{:S(2)}, u32[]{:S(2)}) %collective-permute-start.2) | collective-permute-done | bytes 294944 | tf_op jit(solution)/shard_map/ppermute | solution.py:425
  51.9 3.6 %collective-permute-start.7 = (f32[4,72,128]{2,1,0:T(8,128)}, f32[4,72,128]{2,1,0:T(8,128)S(1)}, u32[]{:S(2)}, u32[]{:S(2)}) collective-permute-start(f32[4,72,128]{2,1,0:T(8,128)} %get-tuple-element.66), channel_id=1, source_target_pairs={{0,32},{8,40},{16,48},{24,56},{32,64},{40,72},{48,80},{56,88},{64,... | collective-permute-start | bytes 442376 | tf_op jit(solution)/shard_map/ppermute | solution.py:429
  55.4 3.5 %collective-permute-done.4.refs_2_ = f32[8,72,128]{2,1,0:T(8,128)S(1)} collective-permute-done((f32[8,72,128]{2,1,0:T(8,128)}, f32[8,72,128]{2,1,0:T(8,128)S(1)}, u32[]{:S(2)}, u32[]{:S(2)}) %collective-permute-start.4) | collective-permute-done | bytes 294944 | tf_op jit(solution)/shard_map/ppermute | solution.py:425
  61.2 6.8 %collective-permute-done.5.refs_3_ = f32[8,72,128]{2,1,0:T(8,128)S(1)} collective-permute-done((f32[8,72,128]{2,1,0:T(8,128)}, f32[8,72,128]{2,1,0:T(8,128)S(1)}, u32[]{:S(2)}, u32[]{:S(2)}) %collective-permute-start.5) | collective-permute-done | bytes 294944 | tf_op jit(solution)/shard_map/ppermute | solution.py:425
  71.0 4.2 %collective-permute-done.7.refs_5_ = f32[4,72,128]{2,1,0:T(8,128)S(1)} collective-permute-done((f32[4,72,128]{2,1,0:T(8,128)}, f32[4,72,128]{2,1,0:T(8,128)S(1)}, u32[]{:S(2)}, u32[]{:S(2)}) %collective-permute-start.7) | collective-permute-done | bytes 147488 | tf_op jit(solution)/shard_map/ppermute | solution.py:429
  77.5 5.2 %collective-permute-start.10 = (f32[4,72,128]{2,1,0:T(8,128)}, f32[4,72,128]{2,1,0:T(8,128)S(1)}, u32[]{:S(2)}, u32[]{:S(2)}) collective-permute-start(f32[4,72,128]{2,1,0:T(8,128)} %get-tuple-element.85), channel_id=1, source_target_pairs={{0,64},{8,72},{16,80},{24,88},{32,96},{40,104},{48,112},{56,120},{... | collective-permute-start | bytes 442376 | tf_op jit(solution)/shard_map/ppermute | solution.py:429
  82.6 8.0 %x_transform.3 = f32[8,2,2,18,8,128]{5,4,3,2,1,0:T(8,128)} custom-call(s32[3]{0:T(128)} %pad_add_fusion.place, f32[32,2,72,128]{3,2,1,0:T(8,128)} %copy-done.2, bf16[9,512,256]{2,1,0:T(8,128)(2,1)} %constant.60.clone.refs_1_.refs_11_), custom_call_target="tpu_custom_call" | custom-call | flops 20000000000 | tf_op jit(solution)/shard_map/x_transform/pallas_call | solution.py:250
  91.4 5.2 %all-to-all-start.1 = ((f32[8,2,2,144,128]{4,3,2,1,0:T(8,128)}), f32[8,2,2,144,128]{4,3,2,1,0:T(8,128)S(1)}, u32[]{:S(2)}, u32[]{:S(2)}) async-start(f32[8,2,2,144,128]{4,3,2,1,0:T(8,128)} %bitcast.11), calls=%async_computation.1 | async-start | bytes 4718592 | tf_op jit(solution)/shard_map/all_to_all | solution.py:421
  96.6 4.2 %collective-permute-start.11 = (f32[4,72,128]{2,1,0:T(8,128)S(1)}, f32[4,72,128]{2,1,0:T(8,128)S(1)}, u32[]{:S(2)}, u32[]{:S(2)}) collective-permute-start(f32[4,72,128]{2,1,0:T(8,128)S(1)} %copy-done.17), channel_id=1, source_target_pairs={{0,48},{8,56},{16,64},{24,72},{32,80},{40,88},{48,96},{56,104},{64... | collective-permute-start | bytes 442376 | tf_op jit(solution)/shard_map/ppermute | solution.py:429
  110.8 5.0 %collective-permute-done.12.refs_8_ = f32[4,72,128]{2,1,0:T(8,128)S(1)} collective-permute-done((f32[4,72,128]{2,1,0:T(8,128)S(1)}, f32[4,72,128]{2,1,0:T(8,128)S(1)}, u32[]{:S(2)}, u32[]{:S(2)}) %collective-permute-start.12) | collective-permute-done | bytes 147488 | tf_op jit(solution)/shard_map/ppermute | solution.py:429
  116.9 4.0 %collective-permute-start.18 = (f32[4,72,128]{2,1,0:T(8,128)S(1)}, f32[4,72,128]{2,1,0:T(8,128)}, u32[]{:S(2)}, u32[]{:S(2)}) collective-permute-start(f32[4,72,128]{2,1,0:T(8,128)S(1)} %copy-done.11), channel_id=1, source_target_pairs={{0,80},{8,88},{16,96},{24,104},{32,112},{40,120},{48,0},{56,8},{64... | collective-permute-start | bytes 442376 | tf_op jit(solution)/shard_map/ppermute | solution.py:429
  120.9 4.6 %collective-permute-done.14.refs_7_ = f32[4,72,128]{2,1,0:T(8,128)} collective-permute-done((f32[4,72,128]{2,1,0:T(8,128)}, f32[4,72,128]{2,1,0:T(8,128)}, u32[]{:S(2)}, u32[]{:S(2)}) %collective-permute-start.14) | collective-permute-done | bytes 147488 | tf_op jit(solution)/shard_map/ppermute | solution.py:429
  125.5 5.4 %x_transform.4.refs_12_ = f32[8,1,2,18,8,128]{5,4,3,2,1,0:T(8,128)} custom-call(s32[3]{0:T(128)} %pad_add_fusion.place, f32[8,72,128]{2,1,0:T(8,128)} %get-tuple-element.61.refs_0_, f32[8,72,128]{2,1,0:T(8,128)} %copy-done.6, f32[8,72,128]{2,1,0:T(8,128)} %copy-done.7, f32[8,72,128]{2,1,0:T(8,128)} %collective-permute-done.2.refs_3_, ...), custom_call_target="tpu_custom_call" | custom-call | flops 20000000000 | tf_op jit(solution)/shard_map/x_transform/pallas_call | solution.py:250
  130.9 5.8 %all-to-all-start.2 = ((f32[8,1,2,144,128]{4,3,2,1,0:T(8,128)}), f32[8,1,2,144,128]{4,3,2,1,0:T(8,128)}, u32[]{:S(2)}, u32[]{:S(2)}) async-start(f32[8,1,2,144,128]{4,3,2,1,0:T(8,128)} %bitcast.12), calls=%async_computation.2 | async-start | bytes 2359296 | tf_op jit(solution)/shard_map/all_to_all | solution.py:421
  137.4 5.4 %x_transform.5 = f32[8,1,2,18,8,128]{5,4,3,2,1,0:T(8,128)} custom-call(s32[3]{0:T(128)} %pad_add_fusion.place, f32[8,72,128]{2,1,0:T(8,128)} %get-tuple-element.72.refs_0_, f32[8,72,128]{2,1,0:T(8,128)} %copy-done.3, f32[8,72,128]{2,1,0:T(8,128)} %copy-done.4, f32[8,72,128]{2,1,0:T(8,128)} %copy-done.5, f32[4,72,128]{2,1,0:T(8,128)} %copy-done.19, ...), custom_call_target="tpu_custom_call" | custom-call | flops 199999995904 | tf_op jit(solution)/shard_map/x_transform/pallas_call | solution.py:250
  142.8 7.8 %all-to-all-done.2.refs_0_ = f32[8,1,2,144,128]{4,3,2,1,0:T(8,128)} async-done(((f32[8,1,2,144,128]{4,3,2,1,0:T(8,128)}), f32[8,1,2,144,128]{4,3,2,1,0:T(8,128)}, u32[]{:S(2)}, u32[]{:S(2)}) %all-to-all-start.2) | async-done | bytes 1179680 | tf_op jit(solution)/shard_map/all_to_all | solution.py:421
  150.6 3.8 %all-to-all-start.3 = ((f32[8,1,2,144,128]{4,3,2,1,0:T(8,128)}), f32[8,1,2,144,128]{4,3,2,1,0:T(8,128)S(1)}, u32[]{:S(2)}, u32[]{:S(2)}) async-start(f32[8,1,2,144,128]{4,3,2,1,0:T(8,128)} %bitcast.13), calls=%async_computation.3 | async-start | bytes 2359296 | tf_op jit(solution)/shard_map/all_to_all | solution.py:421
  154.4 7.4 %y_transform.2.refs_5_ = f32[2,2,144,2000]{3,2,1,0:T(8,128)} custom-call(f32[8,2,2,144,128]{4,3,2,1,0:T(8,128)} %copy-done, f32[2,8,2,128]{3,2,1,0:T(2,128)} %constant.61.clone.refs_1_.refs_2_, bf16[2,512,512]{2,1,0:T(8,128)(2,1)} %constant.62.clone.refs_2_.refs_3_, bf16[4,256,256]{2,1,0:T(8,128)(2,1)} %constant.63.clone.refs_3_.refs_4_), custom_call_target="tpu_custom_call" | custom-call | tf_op jit(solution)/shard_map/y_transform/pallas_call | solution.py:385
  161.8 5.5 %all-to-all-done.3.refs_1_ = f32[8,1,2,144,128]{4,3,2,1,0:T(8,128)S(1)} async-done(((f32[8,1,2,144,128]{4,3,2,1,0:T(8,128)}), f32[8,1,2,144,128]{4,3,2,1,0:T(8,128)S(1)}, u32[]{:S(2)}, u32[]{:S(2)}) %all-to-all-start.3) | async-done | bytes 1179680 | tf_op jit(solution)/shard_map/all_to_all | solution.py:421
  168.3 7.4 %y_transform.3 = f32[2,2,144,2000]{3,2,1,0:T(8,128)} custom-call(f32[8,1,2,144,128]{4,3,2,1,0:T(8,128)} %all-to-all-done.2.refs_0_, f32[8,1,2,144,128]{4,3,2,1,0:T(8,128)} %copy-done.1, f32[2,8,2,128]{3,2,1,0:T(2,128)} %constant.61.clone.refs_1_.refs_2_, bf16[2,512,512]{2,1,0:T(8,128)(2,1)} %constant.62.clone.refs_2_.refs_3_, ...), custom_call_target="tpu_custom_call", output_to_operand_aliasing={{}: (5, {})} | custom-call | tf_op jit(solution)/shard_map/y_transform/pallas_call | solution.py:385
  (83 shorter events, 33.3 us)
Async XLA Ops:
  4.0 73.4 %all-to-all-start = ((f32[32,2,72,128]{3,2,1,0:T(8,128)}), f32[32,2,72,128]{3,2,1,0:T(8,128)S(1)}, u32[]{:S(2)}, u32[]{:S(2)}) async-start(f32[32,2,72,128]{3,2,1,0:T(8,128)} %bitcast.8), calls=%async_computation | async-start | bytes 4718592 | tf_op jit(solution)/shard_map/all_to_all | solution.py:443
  18.9 4.4 %collective-permute-start = (f32[8,72,128]{2,1,0:T(8,128)}, f32[8,72,128]{2,1,0:T(8,128)S(1)}, u32[]{:S(2)}, u32[]{:S(2)}) collective-permute-start(f32[8,72,128]{2,1,0:T(8,128)} %get-tuple-element.62), channel_id=1, source_target_pairs={{0,8},{8,0},{16,24},{24,16},{32,40},{40,32},{48,56},{56,48},{64,72... | collective-permute-start | bytes 884744 | tf_op jit(solution)/shard_map/ppermute | solution.py:425
  19.1 16.2 %collective-permute-start.1 = (f32[8,72,128]{2,1,0:T(8,128)}, f32[8,72,128]{2,1,0:T(8,128)S(1)}, u32[]{:S(2)}, u32[]{:S(2)}) collective-permute-start(f32[8,72,128]{2,1,0:T(8,128)} %get-tuple-element.63), channel_id=1, source_target_pairs={{0,128},{8,136},{16,144},{24,152},{32,160},{40,168},{48,176},{56,1... | collective-permute-start | bytes 884744 | tf_op jit(solution)/shard_map/ppermute | solution.py:425
  19.7 27.9 %collective-permute-start.2 = (f32[8,72,128]{2,1,0:T(8,128)}, f32[8,72,128]{2,1,0:T(8,128)}, u32[]{:S(2)}, u32[]{:S(2)}) collective-permute-start(f32[8,72,128]{2,1,0:T(8,128)} %get-tuple-element.64), channel_id=1, source_target_pairs={{0,136},{8,128},{16,152},{24,144},{32,168},{40,160},{48,184},{56,1... | collective-permute-start | bytes 884744 | tf_op jit(solution)/shard_map/ppermute | solution.py:425
  22.3 33.1 %collective-permute-start.3 = (f32[8,72,128]{2,1,0:T(8,128)}, f32[8,72,128]{2,1,0:T(8,128)S(1)}, u32[]{:S(2)}, u32[]{:S(2)}) collective-permute-start(f32[8,72,128]{2,1,0:T(8,128)} %get-tuple-element.73), channel_id=1, source_target_pairs={{0,8},{8,0},{16,24},{24,16},{32,40},{40,32},{48,56},{56,48},{64,72... | collective-permute-start | bytes 884744 | tf_op jit(solution)/shard_map/ppermute | solution.py:425
  22.8 36.2 %collective-permute-start.4 = (f32[8,72,128]{2,1,0:T(8,128)}, f32[8,72,128]{2,1,0:T(8,128)S(1)}, u32[]{:S(2)}, u32[]{:S(2)}) collective-permute-start(f32[8,72,128]{2,1,0:T(8,128)} %get-tuple-element.74), channel_id=1, source_target_pairs={{0,128},{8,136},{16,144},{24,152},{32,160},{40,168},{48,176},{56,1... | collective-permute-start | bytes 884744 | tf_op jit(solution)/shard_map/ppermute | solution.py:425
  23.3 44.7 %collective-permute-start.5 = (f32[8,72,128]{2,1,0:T(8,128)}, f32[8,72,128]{2,1,0:T(8,128)S(1)}, u32[]{:S(2)}, u32[]{:S(2)}) collective-permute-start(f32[8,72,128]{2,1,0:T(8,128)} %get-tuple-element.75), channel_id=1, source_target_pairs={{0,136},{8,128},{16,152},{24,144},{32,168},{40,160},{48,184},{56,1... | collective-permute-start | bytes 884744 | tf_op jit(solution)/shard_map/ppermute | solution.py:425
  49.9 21.1 %collective-permute-start.6 = (f32[4,72,128]{2,1,0:T(8,128)}, f32[4,72,128]{2,1,0:T(8,128)S(1)}, u32[]{:S(2)}, u32[]{:S(2)}) collective-permute-start(f32[4,72,128]{2,1,0:T(8,128)} %get-tuple-element.65), channel_id=1, source_target_pairs={{0,16},{8,24},{16,32},{24,40},{32,48},{40,56},{48,64},{56,72},{64,... | collective-permute-start | bytes 442376 | tf_op jit(solution)/shard_map/ppermute | solution.py:429
  51.9 23.4 %collective-permute-start.7 = (f32[4,72,128]{2,1,0:T(8,128)}, f32[4,72,128]{2,1,0:T(8,128)S(1)}, u32[]{:S(2)}, u32[]{:S(2)}) collective-permute-start(f32[4,72,128]{2,1,0:T(8,128)} %get-tuple-element.66), channel_id=1, source_target_pairs={{0,32},{8,40},{16,48},{24,56},{32,64},{40,72},{48,80},{56,88},{64,... | collective-permute-start | bytes 442376 | tf_op jit(solution)/shard_map/ppermute | solution.py:429
  55.4 21.4 %collective-permute-start.8 = (f32[4,72,128]{2,1,0:T(8,128)}, f32[4,72,128]{2,1,0:T(8,128)S(1)}, u32[]{:S(2)}, u32[]{:S(2)}) collective-permute-start(f32[4,72,128]{2,1,0:T(8,128)} %get-tuple-element.70), channel_id=1, source_target_pairs={{0,96},{8,104},{16,112},{24,120},{32,0},{40,8},{48,16},{56,24},{64... | collective-permute-start | bytes 442376 | tf_op jit(solution)/shard_map/ppermute | solution.py:429
  59.0 18.5 %collective-permute-start.9 = (f32[4,72,128]{2,1,0:T(8,128)}, f32[4,72,128]{2,1,0:T(8,128)}, u32[]{:S(2)}, u32[]{:S(2)}) collective-permute-start(f32[4,72,128]{2,1,0:T(8,128)} %get-tuple-element.71), channel_id=1, source_target_pairs={{0,112},{8,120},{16,0},{24,8},{32,16},{40,24},{48,32},{56,40},{64,... | collective-permute-start | bytes 442376 | tf_op jit(solution)/shard_map/ppermute | solution.py:429
  77.5 13.2 %collective-permute-start.10 = (f32[4,72,128]{2,1,0:T(8,128)}, f32[4,72,128]{2,1,0:T(8,128)S(1)}, u32[]{:S(2)}, u32[]{:S(2)}) collective-permute-start(f32[4,72,128]{2,1,0:T(8,128)} %get-tuple-element.85), channel_id=1, source_target_pairs={{0,64},{8,72},{16,80},{24,88},{32,96},{40,104},{48,112},{56,120},{... | collective-permute-start | bytes 442376 | tf_op jit(solution)/shard_map/ppermute | solution.py:429
  91.4 39.5 %all-to-all-start.1 = ((f32[8,2,2,144,128]{4,3,2,1,0:T(8,128)}), f32[8,2,2,144,128]{4,3,2,1,0:T(8,128)S(1)}, u32[]{:S(2)}, u32[]{:S(2)}) async-start(f32[8,2,2,144,128]{4,3,2,1,0:T(8,128)} %bitcast.11), calls=%async_computation.1 | async-start | bytes 4718592 | tf_op jit(solution)/shard_map/all_to_all | solution.py:421
  96.6 12.9 %collective-permute-start.11 = (f32[4,72,128]{2,1,0:T(8,128)S(1)}, f32[4,72,128]{2,1,0:T(8,128)S(1)}, u32[]{:S(2)}, u32[]{:S(2)}) collective-permute-start(f32[4,72,128]{2,1,0:T(8,128)S(1)} %copy-done.17), channel_id=1, source_target_pairs={{0,48},{8,56},{16,64},{24,72},{32,80},{40,88},{48,96},{56,104},{64... | collective-permute-start | bytes 442376 | tf_op jit(solution)/shard_map/ppermute | solution.py:429
  100.8 15.0 %collective-permute-start.12 = (f32[4,72,128]{2,1,0:T(8,128)S(1)}, f32[4,72,128]{2,1,0:T(8,128)S(1)}, u32[]{:S(2)}, u32[]{:S(2)}) collective-permute-start(f32[4,72,128]{2,1,0:T(8,128)S(1)} %copy-done.16), channel_id=1, source_target_pairs={{0,80},{8,88},{16,96},{24,104},{32,112},{40,120},{48,0},{56,8},{64... | collective-permute-start | bytes 442376 | tf_op jit(solution)/shard_map/ppermute | solution.py:429
  101.7 15.2 %collective-permute-start.13 = (f32[4,72,128]{2,1,0:T(8,128)}, f32[4,72,128]{2,1,0:T(8,128)S(1)}, u32[]{:S(2)}, u32[]{:S(2)}) collective-permute-start(f32[4,72,128]{2,1,0:T(8,128)} %get-tuple-element.102), channel_id=1, source_target_pairs={{0,32},{8,40},{16,48},{24,56},{32,64},{40,72},{48,80},{56,88},{64,... | collective-permute-start | bytes 442376 | tf_op jit(solution)/shard_map/ppermute | solution.py:429
  103.3 22.2 %collective-permute-start.14 = (f32[4,72,128]{2,1,0:T(8,128)}, f32[4,72,128]{2,1,0:T(8,128)}, u32[]{:S(2)}, u32[]{:S(2)}) collective-permute-start(f32[4,72,128]{2,1,0:T(8,128)} %get-tuple-element.103), channel_id=1, source_target_pairs={{0,64},{8,72},{16,80},{24,88},{32,96},{40,104},{48,112},{56,120},{... | collective-permute-start | bytes 442376 | tf_op jit(solution)/shard_map/ppermute | solution.py:429
  106.0 24.9 %collective-permute-start.15 = (f32[4,72,128]{2,1,0:T(8,128)S(1)}, f32[4,72,128]{2,1,0:T(8,128)}, u32[]{:S(2)}, u32[]{:S(2)}) collective-permute-start(f32[4,72,128]{2,1,0:T(8,128)S(1)} %copy-done.15), channel_id=1, source_target_pairs={{0,96},{8,104},{16,112},{24,120},{32,0},{40,8},{48,16},{56,24},{64... | collective-permute-start | bytes 442376 | tf_op jit(solution)/shard_map/ppermute | solution.py:429
  109.6 27.1 %collective-permute-start.16 = (f32[4,72,128]{2,1,0:T(8,128)S(1)}, f32[4,72,128]{2,1,0:T(8,128)S(1)}, u32[]{:S(2)}, u32[]{:S(2)}) collective-permute-start(f32[4,72,128]{2,1,0:T(8,128)S(1)} %copy-done.13), channel_id=1, source_target_pairs={{0,16},{8,24},{16,32},{24,40},{32,48},{40,56},{48,64},{56,72},{64,... | collective-permute-start | bytes 442376 | tf_op jit(solution)/shard_map/ppermute | solution.py:429
  115.8 20.9 %collective-permute-start.17 = (f32[4,72,128]{2,1,0:T(8,128)S(1)}, f32[4,72,128]{2,1,0:T(8,128)S(1)}, u32[]{:S(2)}, u32[]{:S(2)}) collective-permute-start(f32[4,72,128]{2,1,0:T(8,128)S(1)} %copy-done.12), channel_id=1, source_target_pairs={{0,48},{8,56},{16,64},{24,72},{32,80},{40,88},{48,96},{56,104},{64... | collective-permute-start | bytes 442376 | tf_op jit(solution)/shard_map/ppermute | solution.py:429
  116.9 19.8 %collective-permute-start.18 = (f32[4,72,128]{2,1,0:T(8,128)S(1)}, f32[4,72,128]{2,1,0:T(8,128)}, u32[]{:S(2)}, u32[]{:S(2)}) collective-permute-start(f32[4,72,128]{2,1,0:T(8,128)S(1)} %copy-done.11), channel_id=1, source_target_pairs={{0,80},{8,88},{16,96},{24,104},{32,112},{40,120},{48,0},{56,8},{64... | collective-permute-start | bytes 442376 | tf_op jit(solution)/shard_map/ppermute | solution.py:429
  125.5 11.3 %collective-permute-start.19 = (f32[4,72,128]{2,1,0:T(8,128)S(1)}, f32[4,72,128]{2,1,0:T(8,128)}, u32[]{:S(2)}, u32[]{:S(2)}) collective-permute-start(f32[4,72,128]{2,1,0:T(8,128)S(1)} %copy-done.9), channel_id=1, source_target_pairs={{0,112},{8,120},{16,0},{24,8},{32,16},{40,24},{48,32},{56,40},{64,... | collective-permute-start | bytes 442376 | tf_op jit(solution)/shard_map/ppermute | solution.py:429
  130.9 19.7 %all-to-all-start.2 = ((f32[8,1,2,144,128]{4,3,2,1,0:T(8,128)}), f32[8,1,2,144,128]{4,3,2,1,0:T(8,128)}, u32[]{:S(2)}, u32[]{:S(2)}) async-start(f32[8,1,2,144,128]{4,3,2,1,0:T(8,128)} %bitcast.12), calls=%async_computation.2 | async-start | bytes 2359296 | tf_op jit(solution)/shard_map/all_to_all | solution.py:421
  150.6 16.7 %all-to-all-start.3 = ((f32[8,1,2,144,128]{4,3,2,1,0:T(8,128)}), f32[8,1,2,144,128]{4,3,2,1,0:T(8,128)S(1)}, u32[]{:S(2)}, u32[]{:S(2)}) async-start(f32[8,1,2,144,128]{4,3,2,1,0:T(8,128)} %bitcast.13), calls=%async_computation.3 | async-start | bytes 2359296 | tf_op jit(solution)/shard_map/all_to_all | solution.py:421
  (24 other events, 286.1 us)

commit v4 on v3

--- a/solution.py
+++ b/solution.py
@@ -239,8 +239,13 @@
                 total = total.reshape(NJ, 2, 2, 8, LANES)
                 for group, number in enumerate((0, 9) if q == 0 else (q, 18 - q)):
                     out[:, half, :, number] = total[:, group]
-            stores.append(pltpu.make_async_copy(out.at[:, half], result.at[:, half], out_sem))
-            stores[half].start()
+                ready = {4: ((0, 5), (14, 4)), 8: ((5, 9),)}.get(q, ())
+                for low, count in ready:
+                    classes = pl.ds(low, count)
+                    stores.append(
+                        pltpu.make_async_copy(out.at[:, half, :, classes], result.at[:, half, :, classes], out_sem)
+                    )
+                    stores[-1].start()
         for store in stores:
             store.wait()
 

time: 178 us -> 178 us (level)
  no operation moved by 1% of the time
where the time goes in v4:
time: 178 us; the launch traced here: 177 us
  waiting for transfers between devices  63.9 us (36%)
  starting transfers between devices  63 us (35%)
  Pallas kernels  44.7 us (25%)
  local copies, waits for them, and re-layouts  4.38 us (2%)
    ppermute x6, waiting for transfers between devices, over_xh(): lax.ppermute(part, 'gx', shift(dh, 0, dc))  32.2 us
    ppermute x14, starting transfers between devices, over_z(): lax.ppermute(sends[dz - 1], 'gx', shift(0, dz, 0))  30.7 us
    pallas_call x3, Pallas kernels, x_transform(): pl.pallas_call(kernel, in_specs=[pl.BlockSpec(memory_space=pltpu.SMEM)] +...  18.5 us
    ppermute x14, waiting for transfers between devices, over_z(): lax.ppermute(sends[dz - 1], 'gx', shift(0, dz, 0))  16.7 us
    all_to_all x3, waiting for transfers between devices, over_y(): return lax.all_to_all(blocks, 'gy', split_axis=0, concat_axis=0, tiled=True)  15 us
    all_to_all x3, starting transfers between devices, over_y(): return lax.all_to_all(blocks, 'gy', split_axis=0, concat_axis=0, tiled=True)  14.8 us
    pallas_call x2, Pallas kernels, y_transform(): pl.pallas_call(functools.partial(y_kernel, len(arrays), field), in_specs=...  14.7 us
    all_to_all x1, starting transfers between devices, body(): first = lax.all_to_all(first, 'gx', split_axis=0, concat_axis=0, tiled=True)  10.7 us
  transfers between devices with their start and end apart: 24, of which 11 were waited for; matrix products, arithmetic and copies ran while one was open for 0% of the time, Pallas kernels for 19%

profile of v4, /device:TPU:68, one launch (start us, length us, event | category | flops | bytes accessed | tf_op | source)
XLA Modules:
  0.0 177.1 jit_solution(7951828186116542640)
XLA Ops:
  0.6 3.5 %pack.2.refs_0_ = f32[2,8,2,2,72,128]{5,4,3,2,1,0:T(8,128)} custom-call(s32[3]{0:T(128)} %broadcast_1_place.2.place, f32[2,8,2,2,72,250]{5,4,3,2,1,0:T(8,128)} %bitcast.9), custom_call_target="tpu_custom_call" | custom-call | tf_op jit(solution)/shard_map/pack/pallas_call | solution.py:120
  4.0 10.7 %all-to-all-start = ((f32[32,2,72,128]{3,2,1,0:T(8,128)}), f32[32,2,72,128]{3,2,1,0:T(8,128)S(1)}, u32[]{:S(2)}, u32[]{:S(2)}) async-start(f32[32,2,72,128]{3,2,1,0:T(8,128)} %bitcast.8), calls=%async_computation | async-start | bytes 4718592 | tf_op jit(solution)/shard_map/all_to_all | solution.py:448
  15.4 3.5 %pack.3 = (f32[8,72,128]{2,1,0:T(8,128)}, f32[8,72,128]{2,1,0:T(8,128)}, f32[8,72,128]{2,1,0:T(8,128)}, f32[8,72,128]{2,1,0:T(8,128)}, f32[8,72,128]{2,1,0:T(8,1...) custom-call(s32[3]{0:T(128)} %pad_add_fusion.place, f32[2,8,2,2,72,250]{5,4,3,2,1,0:T(8,128)} %bitcast.10, ...), custom_call_target="tpu_custom_call" | custom-call | tf_op jit(solution)/shard_map/pack/pallas_call | solution.py:120
  25.7 9.6 %collective-permute-done.1.refs_2_ = f32[8,72,128]{2,1,0:T(8,128)S(1)} collective-permute-done((f32[8,72,128]{2,1,0:T(8,128)}, f32[8,72,128]{2,1,0:T(8,128)S(1)}, u32[]{:S(2)}, u32[]{:S(2)}) %collective-permute-start.1) | collective-permute-done | bytes 294944 | tf_op jit(solution)/shard_map/ppermute | solution.py:430
  35.3 12.3 %collective-permute-done.2.refs_3_ = f32[8,72,128]{2,1,0:T(8,128)} collective-permute-done((f32[8,72,128]{2,1,0:T(8,128)}, f32[8,72,128]{2,1,0:T(8,128)}, u32[]{:S(2)}, u32[]{:S(2)}) %collective-permute-start.2) | collective-permute-done | bytes 294944 | tf_op jit(solution)/shard_map/ppermute | solution.py:430
  51.9 3.6 %collective-permute-start.7 = (f32[4,72,128]{2,1,0:T(8,128)}, f32[4,72,128]{2,1,0:T(8,128)S(1)}, u32[]{:S(2)}, u32[]{:S(2)}) collective-permute-start(f32[4,72,128]{2,1,0:T(8,128)} %get-tuple-element.66), channel_id=1, source_target_pairs={{0,32},{8,40},{16,48},{24,56},{32,64},{40,72},{48,80},{56,88},{64,... | collective-permute-start | bytes 442376 | tf_op jit(solution)/shard_map/ppermute | solution.py:434
  55.4 3.5 %collective-permute-done.4.refs_2_ = f32[8,72,128]{2,1,0:T(8,128)S(1)} collective-permute-done((f32[8,72,128]{2,1,0:T(8,128)}, f32[8,72,128]{2,1,0:T(8,128)S(1)}, u32[]{:S(2)}, u32[]{:S(2)}) %collective-permute-start.4) | collective-permute-done | bytes 294944 | tf_op jit(solution)/shard_map/ppermute | solution.py:430
  61.2 6.8 %collective-permute-done.5.refs_3_ = f32[8,72,128]{2,1,0:T(8,128)S(1)} collective-permute-done((f32[8,72,128]{2,1,0:T(8,128)}, f32[8,72,128]{2,1,0:T(8,128)S(1)}, u32[]{:S(2)}, u32[]{:S(2)}) %collective-permute-start.5) | collective-permute-done | bytes 294944 | tf_op jit(solution)/shard_map/ppermute | solution.py:430
  71.0 4.2 %collective-permute-done.7.refs_5_ = f32[4,72,128]{2,1,0:T(8,128)S(1)} collective-permute-done((f32[4,72,128]{2,1,0:T(8,128)}, f32[4,72,128]{2,1,0:T(8,128)S(1)}, u32[]{:S(2)}, u32[]{:S(2)}) %collective-permute-start.7) | collective-permute-done | bytes 147488 | tf_op jit(solution)/shard_map/ppermute | solution.py:434
  77.5 5.2 %collective-permute-start.10 = (f32[4,72,128]{2,1,0:T(8,128)}, f32[4,72,128]{2,1,0:T(8,128)S(1)}, u32[]{:S(2)}, u32[]{:S(2)}) collective-permute-start(f32[4,72,128]{2,1,0:T(8,128)} %get-tuple-element.85), channel_id=1, source_target_pairs={{0,64},{8,72},{16,80},{24,88},{32,96},{40,104},{48,112},{56,120},{... | collective-permute-start | bytes 442376 | tf_op jit(solution)/shard_map/ppermute | solution.py:434
  82.6 8.1 %x_transform.3 = f32[8,2,2,18,8,128]{5,4,3,2,1,0:T(8,128)} custom-call(s32[3]{0:T(128)} %pad_add_fusion.place, f32[32,2,72,128]{3,2,1,0:T(8,128)} %copy-done.2, bf16[9,512,256]{2,1,0:T(8,128)(2,1)} %constant.60.clone.refs_1_.refs_11_), custom_call_target="tpu_custom_call" | custom-call | flops 20000000000 | tf_op jit(solution)/shard_map/x_transform/pallas_call | solution.py:255
  91.5 5.2 %all-to-all-start.1 = ((f32[8,2,2,144,128]{4,3,2,1,0:T(8,128)}), f32[8,2,2,144,128]{4,3,2,1,0:T(8,128)S(1)}, u32[]{:S(2)}, u32[]{:S(2)}) async-start(f32[8,2,2,144,128]{4,3,2,1,0:T(8,128)} %bitcast.11), calls=%async_computation.1 | async-start | bytes 4718592 | tf_op jit(solution)/shard_map/all_to_all | solution.py:426
  96.7 4.1 %collective-permute-start.11 = (f32[4,72,128]{2,1,0:T(8,128)S(1)}, f32[4,72,128]{2,1,0:T(8,128)S(1)}, u32[]{:S(2)}, u32[]{:S(2)}) collective-permute-start(f32[4,72,128]{2,1,0:T(8,128)S(1)} %copy-done.17), channel_id=1, source_target_pairs={{0,48},{8,56},{16,64},{24,72},{32,80},{40,88},{48,96},{56,104},{64... | collective-permute-start | bytes 442376 | tf_op jit(solution)/shard_map/ppermute | solution.py:434
  110.9 5.0 %collective-permute-done.12.refs_8_ = f32[4,72,128]{2,1,0:T(8,128)S(1)} collective-permute-done((f32[4,72,128]{2,1,0:T(8,128)S(1)}, f32[4,72,128]{2,1,0:T(8,128)S(1)}, u32[]{:S(2)}, u32[]{:S(2)}) %collective-permute-start.12) | collective-permute-done | bytes 147488 | tf_op jit(solution)/shard_map/ppermute | solution.py:434
  116.0 5.1 %collective-permute-start.18 = (f32[4,72,128]{2,1,0:T(8,128)S(1)}, f32[4,72,128]{2,1,0:T(8,128)}, u32[]{:S(2)}, u32[]{:S(2)}) collective-permute-start(f32[4,72,128]{2,1,0:T(8,128)S(1)} %copy-done.11), channel_id=1, source_target_pairs={{0,80},{8,88},{16,96},{24,104},{32,112},{40,120},{48,0},{56,8},{64... | collective-permute-start | bytes 442376 | tf_op jit(solution)/shard_map/ppermute | solution.py:434
  121.1 4.3 %collective-permute-done.14.refs_7_ = f32[4,72,128]{2,1,0:T(8,128)} collective-permute-done((f32[4,72,128]{2,1,0:T(8,128)}, f32[4,72,128]{2,1,0:T(8,128)}, u32[]{:S(2)}, u32[]{:S(2)}) %collective-permute-start.14) | collective-permute-done | bytes 147488 | tf_op jit(solution)/shard_map/ppermute | solution.py:434
  125.4 5.2 %x_transform.4.refs_12_ = f32[8,1,2,18,8,128]{5,4,3,2,1,0:T(8,128)} custom-call(s32[3]{0:T(128)} %pad_add_fusion.place, f32[8,72,128]{2,1,0:T(8,128)} %get-tuple-element.61.refs_0_, f32[8,72,128]{2,1,0:T(8,128)} %copy-done.6, f32[8,72,128]{2,1,0:T(8,128)} %copy-done.7, f32[8,72,128]{2,1,0:T(8,128)} %collective-permute-done.2.refs_3_, ...), custom_call_target="tpu_custom_call" | custom-call | flops 20000000000 | tf_op jit(solution)/shard_map/x_transform/pallas_call | solution.py:255
  130.6 5.8 %all-to-all-start.2 = ((f32[8,1,2,144,128]{4,3,2,1,0:T(8,128)}), f32[8,1,2,144,128]{4,3,2,1,0:T(8,128)}, u32[]{:S(2)}, u32[]{:S(2)}) async-start(f32[8,1,2,144,128]{4,3,2,1,0:T(8,128)} %bitcast.12), calls=%async_computation.2 | async-start | bytes 2359296 | tf_op jit(solution)/shard_map/all_to_all | solution.py:426
  137.1 5.2 %x_transform.5 = f32[8,1,2,18,8,128]{5,4,3,2,1,0:T(8,128)} custom-call(s32[3]{0:T(128)} %pad_add_fusion.place, f32[8,72,128]{2,1,0:T(8,128)} %get-tuple-element.72.refs_0_, f32[8,72,128]{2,1,0:T(8,128)} %copy-done.3, f32[8,72,128]{2,1,0:T(8,128)} %copy-done.4, f32[8,72,128]{2,1,0:T(8,128)} %copy-done.5, f32[4,72,128]{2,1,0:T(8,128)} %copy-done.19, ...), custom_call_target="tpu_custom_call" | custom-call | flops 199999995904 | tf_op jit(solution)/shard_map/x_transform/pallas_call | solution.py:255
  142.3 8.4 %all-to-all-done.2.refs_0_ = f32[8,1,2,144,128]{4,3,2,1,0:T(8,128)} async-done(((f32[8,1,2,144,128]{4,3,2,1,0:T(8,128)}), f32[8,1,2,144,128]{4,3,2,1,0:T(8,128)}, u32[]{:S(2)}, u32[]{:S(2)}) %all-to-all-start.2) | async-done | bytes 1179680 | tf_op jit(solution)/shard_map/all_to_all | solution.py:426
  150.7 3.8 %all-to-all-start.3 = ((f32[8,1,2,144,128]{4,3,2,1,0:T(8,128)}), f32[8,1,2,144,128]{4,3,2,1,0:T(8,128)S(1)}, u32[]{:S(2)}, u32[]{:S(2)}) async-start(f32[8,1,2,144,128]{4,3,2,1,0:T(8,128)} %bitcast.13), calls=%async_computation.3 | async-start | bytes 2359296 | tf_op jit(solution)/shard_map/all_to_all | solution.py:426
  154.5 7.4 %y_transform.2.refs_5_ = f32[2,2,144,2000]{3,2,1,0:T(8,128)} custom-call(f32[8,2,2,144,128]{4,3,2,1,0:T(8,128)} %copy-done, f32[2,8,2,128]{3,2,1,0:T(2,128)} %constant.61.clone.refs_1_.refs_2_, bf16[2,512,512]{2,1,0:T(8,128)(2,1)} %constant.62.clone.refs_2_.refs_3_, bf16[4,256,256]{2,1,0:T(8,128)(2,1)} %constant.63.clone.refs_3_.refs_4_), custom_call_target="tpu_custom_call" | custom-call | tf_op jit(solution)/shard_map/y_transform/pallas_call | solution.py:390
  161.8 6.6 %all-to-all-done.3.refs_1_ = f32[8,1,2,144,128]{4,3,2,1,0:T(8,128)S(1)} async-done(((f32[8,1,2,144,128]{4,3,2,1,0:T(8,128)}), f32[8,1,2,144,128]{4,3,2,1,0:T(8,128)S(1)}, u32[]{:S(2)}, u32[]{:S(2)}) %all-to-all-start.3) | async-done | bytes 1179680 | tf_op jit(solution)/shard_map/all_to_all | solution.py:426
  169.5 7.4 %y_transform.3 = f32[2,2,144,2000]{3,2,1,0:T(8,128)} custom-call(f32[8,1,2,144,128]{4,3,2,1,0:T(8,128)} %all-to-all-done.2.refs_0_, f32[8,1,2,144,128]{4,3,2,1,0:T(8,128)} %copy-done.1, f32[2,8,2,128]{3,2,1,0:T(2,128)} %constant.61.clone.refs_1_.refs_2_, bf16[2,512,512]{2,1,0:T(8,128)(2,1)} %constant.62.clone.refs_2_.refs_3_, ...), custom_call_target="tpu_custom_call", output_to_operand_aliasing={{}: (5, {})} | custom-call | tf_op jit(solution)/shard_map/y_transform/pallas_call | solution.py:390
  (83 shorter events, 32.3 us)
Async XLA Ops:
  4.0 73.4 %all-to-all-start = ((f32[32,2,72,128]{3,2,1,0:T(8,128)}), f32[32,2,72,128]{3,2,1,0:T(8,128)S(1)}, u32[]{:S(2)}, u32[]{:S(2)}) async-start(f32[32,2,72,128]{3,2,1,0:T(8,128)} %bitcast.8), calls=%async_computation | async-start | bytes 4718592 | tf_op jit(solution)/shard_map/all_to_all | solution.py:448
  18.9 4.4 %collective-permute-start = (f32[8,72,128]{2,1,0:T(8,128)}, f32[8,72,128]{2,1,0:T(8,128)S(1)}, u32[]{:S(2)}, u32[]{:S(2)}) collective-permute-start(f32[8,72,128]{2,1,0:T(8,128)} %get-tuple-element.62), channel_id=1, source_target_pairs={{0,8},{8,0},{16,24},{24,16},{32,40},{40,32},{48,56},{56,48},{64,72... | collective-permute-start | bytes 884744 | tf_op jit(solution)/shard_map/ppermute | solution.py:430
  19.1 16.2 %collective-permute-start.1 = (f32[8,72,128]{2,1,0:T(8,128)}, f32[8,72,128]{2,1,0:T(8,128)S(1)}, u32[]{:S(2)}, u32[]{:S(2)}) collective-permute-start(f32[8,72,128]{2,1,0:T(8,128)} %get-tuple-element.63), channel_id=1, source_target_pairs={{0,128},{8,136},{16,144},{24,152},{32,160},{40,168},{48,176},{56,1... | collective-permute-start | bytes 884744 | tf_op jit(solution)/shard_map/ppermute | solution.py:430
  19.7 27.9 %collective-permute-start.2 = (f32[8,72,128]{2,1,0:T(8,128)}, f32[8,72,128]{2,1,0:T(8,128)}, u32[]{:S(2)}, u32[]{:S(2)}) collective-permute-start(f32[8,72,128]{2,1,0:T(8,128)} %get-tuple-element.64), channel_id=1, source_target_pairs={{0,136},{8,128},{16,152},{24,144},{32,168},{40,160},{48,184},{56,1... | collective-permute-start | bytes 884744 | tf_op jit(solution)/shard_map/ppermute | solution.py:430
  22.3 33.1 %collective-permute-start.3 = (f32[8,72,128]{2,1,0:T(8,128)}, f32[8,72,128]{2,1,0:T(8,128)S(1)}, u32[]{:S(2)}, u32[]{:S(2)}) collective-permute-start(f32[8,72,128]{2,1,0:T(8,128)} %get-tuple-element.73), channel_id=1, source_target_pairs={{0,8},{8,0},{16,24},{24,16},{32,40},{40,32},{48,56},{56,48},{64,72... | collective-permute-start | bytes 884744 | tf_op jit(solution)/shard_map/ppermute | solution.py:430
  22.8 36.2 %collective-permute-start.4 = (f32[8,72,128]{2,1,0:T(8,128)}, f32[8,72,128]{2,1,0:T(8,128)S(1)}, u32[]{:S(2)}, u32[]{:S(2)}) collective-permute-start(f32[8,72,128]{2,1,0:T(8,128)} %get-tuple-element.74), channel_id=1, source_target_pairs={{0,128},{8,136},{16,144},{24,152},{32,160},{40,168},{48,176},{56,1... | collective-permute-start | bytes 884744 | tf_op jit(solution)/shard_map/ppermute | solution.py:430
  23.3 44.7 %collective-permute-start.5 = (f32[8,72,128]{2,1,0:T(8,128)}, f32[8,72,128]{2,1,0:T(8,128)S(1)}, u32[]{:S(2)}, u32[]{:S(2)}) collective-permute-start(f32[8,72,128]{2,1,0:T(8,128)} %get-tuple-element.75), channel_id=1, source_target_pairs={{0,136},{8,128},{16,152},{24,144},{32,168},{40,160},{48,184},{56,1... | collective-permute-start | bytes 884744 | tf_op jit(solution)/shard_map/ppermute | solution.py:430
  49.9 21.1 %collective-permute-start.6 = (f32[4,72,128]{2,1,0:T(8,128)}, f32[4,72,128]{2,1,0:T(8,128)S(1)}, u32[]{:S(2)}, u32[]{:S(2)}) collective-permute-start(f32[4,72,128]{2,1,0:T(8,128)} %get-tuple-element.65), channel_id=1, source_target_pairs={{0,16},{8,24},{16,32},{24,40},{32,48},{40,56},{48,64},{56,72},{64,... | collective-permute-start | bytes 442376 | tf_op jit(solution)/shard_map/ppermute | solution.py:434
  51.9 23.4 %collective-permute-start.7 = (f32[4,72,128]{2,1,0:T(8,128)}, f32[4,72,128]{2,1,0:T(8,128)S(1)}, u32[]{:S(2)}, u32[]{:S(2)}) collective-permute-start(f32[4,72,128]{2,1,0:T(8,128)} %get-tuple-element.66), channel_id=1, source_target_pairs={{0,32},{8,40},{16,48},{24,56},{32,64},{40,72},{48,80},{56,88},{64,... | collective-permute-start | bytes 442376 | tf_op jit(solution)/shard_map/ppermute | solution.py:434
  55.4 21.4 %collective-permute-start.8 = (f32[4,72,128]{2,1,0:T(8,128)}, f32[4,72,128]{2,1,0:T(8,128)S(1)}, u32[]{:S(2)}, u32[]{:S(2)}) collective-permute-start(f32[4,72,128]{2,1,0:T(8,128)} %get-tuple-element.70), channel_id=1, source_target_pairs={{0,96},{8,104},{16,112},{24,120},{32,0},{40,8},{48,16},{56,24},{64... | collective-permute-start | bytes 442376 | tf_op jit(solution)/shard_map/ppermute | solution.py:434
  59.0 18.5 %collective-permute-start.9 = (f32[4,72,128]{2,1,0:T(8,128)}, f32[4,72,128]{2,1,0:T(8,128)}, u32[]{:S(2)}, u32[]{:S(2)}) collective-permute-start(f32[4,72,128]{2,1,0:T(8,128)} %get-tuple-element.71), channel_id=1, source_target_pairs={{0,112},{8,120},{16,0},{24,8},{32,16},{40,24},{48,32},{56,40},{64,... | collective-permute-start | bytes 442376 | tf_op jit(solution)/shard_map/ppermute | solution.py:434
  77.5 13.3 %collective-permute-start.10 = (f32[4,72,128]{2,1,0:T(8,128)}, f32[4,72,128]{2,1,0:T(8,128)S(1)}, u32[]{:S(2)}, u32[]{:S(2)}) collective-permute-start(f32[4,72,128]{2,1,0:T(8,128)} %get-tuple-element.85), channel_id=1, source_target_pairs={{0,64},{8,72},{16,80},{24,88},{32,96},{40,104},{48,112},{56,120},{... | collective-permute-start | bytes 442376 | tf_op jit(solution)/shard_map/ppermute | solution.py:434
  91.5 39.1 %all-to-all-start.1 = ((f32[8,2,2,144,128]{4,3,2,1,0:T(8,128)}), f32[8,2,2,144,128]{4,3,2,1,0:T(8,128)S(1)}, u32[]{:S(2)}, u32[]{:S(2)}) async-start(f32[8,2,2,144,128]{4,3,2,1,0:T(8,128)} %bitcast.11), calls=%async_computation.1 | async-start | bytes 4718592 | tf_op jit(solution)/shard_map/all_to_all | solution.py:426
  96.7 12.9 %collective-permute-start.11 = (f32[4,72,128]{2,1,0:T(8,128)S(1)}, f32[4,72,128]{2,1,0:T(8,128)S(1)}, u32[]{:S(2)}, u32[]{:S(2)}) collective-permute-start(f32[4,72,128]{2,1,0:T(8,128)S(1)} %copy-done.17), channel_id=1, source_target_pairs={{0,48},{8,56},{16,64},{24,72},{32,80},{40,88},{48,96},{56,104},{64... | collective-permute-start | bytes 442376 | tf_op jit(solution)/shard_map/ppermute | solution.py:434
  100.8 15.1 %collective-permute-start.12 = (f32[4,72,128]{2,1,0:T(8,128)S(1)}, f32[4,72,128]{2,1,0:T(8,128)S(1)}, u32[]{:S(2)}, u32[]{:S(2)}) collective-permute-start(f32[4,72,128]{2,1,0:T(8,128)S(1)} %copy-done.16), channel_id=1, source_target_pairs={{0,80},{8,88},{16,96},{24,104},{32,112},{40,120},{48,0},{56,8},{64... | collective-permute-start | bytes 442376 | tf_op jit(solution)/shard_map/ppermute | solution.py:434
  101.9 14.1 %collective-permute-start.13 = (f32[4,72,128]{2,1,0:T(8,128)}, f32[4,72,128]{2,1,0:T(8,128)S(1)}, u32[]{:S(2)}, u32[]{:S(2)}) collective-permute-start(f32[4,72,128]{2,1,0:T(8,128)} %get-tuple-element.102), channel_id=1, source_target_pairs={{0,32},{8,40},{16,48},{24,56},{32,64},{40,72},{48,80},{56,88},{64,... | collective-permute-start | bytes 442376 | tf_op jit(solution)/shard_map/ppermute | solution.py:434
  103.3 22.1 %collective-permute-start.14 = (f32[4,72,128]{2,1,0:T(8,128)}, f32[4,72,128]{2,1,0:T(8,128)}, u32[]{:S(2)}, u32[]{:S(2)}) collective-permute-start(f32[4,72,128]{2,1,0:T(8,128)} %get-tuple-element.103), channel_id=1, source_target_pairs={{0,64},{8,72},{16,80},{24,88},{32,96},{40,104},{48,112},{56,120},{... | collective-permute-start | bytes 442376 | tf_op jit(solution)/shard_map/ppermute | solution.py:434
  106.0 24.6 %collective-permute-start.15 = (f32[4,72,128]{2,1,0:T(8,128)S(1)}, f32[4,72,128]{2,1,0:T(8,128)}, u32[]{:S(2)}, u32[]{:S(2)}) collective-permute-start(f32[4,72,128]{2,1,0:T(8,128)S(1)} %copy-done.15), channel_id=1, source_target_pairs={{0,96},{8,104},{16,112},{24,120},{32,0},{40,8},{48,16},{56,24},{64... | collective-permute-start | bytes 442376 | tf_op jit(solution)/shard_map/ppermute | solution.py:434
  109.7 26.7 %collective-permute-start.16 = (f32[4,72,128]{2,1,0:T(8,128)S(1)}, f32[4,72,128]{2,1,0:T(8,128)S(1)}, u32[]{:S(2)}, u32[]{:S(2)}) collective-permute-start(f32[4,72,128]{2,1,0:T(8,128)S(1)} %copy-done.13), channel_id=1, source_target_pairs={{0,16},{8,24},{16,32},{24,40},{32,48},{40,56},{48,64},{56,72},{64,... | collective-permute-start | bytes 442376 | tf_op jit(solution)/shard_map/ppermute | solution.py:434
  116.0 20.5 %collective-permute-start.17 = (f32[4,72,128]{2,1,0:T(8,128)S(1)}, f32[4,72,128]{2,1,0:T(8,128)S(1)}, u32[]{:S(2)}, u32[]{:S(2)}) collective-permute-start(f32[4,72,128]{2,1,0:T(8,128)S(1)} %copy-done.12), channel_id=1, source_target_pairs={{0,48},{8,56},{16,64},{24,72},{32,80},{40,88},{48,96},{56,104},{64... | collective-permute-start | bytes 442376 | tf_op jit(solution)/shard_map/ppermute | solution.py:434
  116.0 20.4 %collective-permute-start.18 = (f32[4,72,128]{2,1,0:T(8,128)S(1)}, f32[4,72,128]{2,1,0:T(8,128)}, u32[]{:S(2)}, u32[]{:S(2)}) collective-permute-start(f32[4,72,128]{2,1,0:T(8,128)S(1)} %copy-done.11), channel_id=1, source_target_pairs={{0,80},{8,88},{16,96},{24,104},{32,112},{40,120},{48,0},{56,8},{64... | collective-permute-start | bytes 442376 | tf_op jit(solution)/shard_map/ppermute | solution.py:434
  125.4 11.1 %collective-permute-start.19 = (f32[4,72,128]{2,1,0:T(8,128)S(1)}, f32[4,72,128]{2,1,0:T(8,128)}, u32[]{:S(2)}, u32[]{:S(2)}) collective-permute-start(f32[4,72,128]{2,1,0:T(8,128)S(1)} %copy-done.9), channel_id=1, source_target_pairs={{0,112},{8,120},{16,0},{24,8},{32,16},{40,24},{48,32},{56,40},{64,... | collective-permute-start | bytes 442376 | tf_op jit(solution)/shard_map/ppermute | solution.py:434
  130.6 20.1 %all-to-all-start.2 = ((f32[8,1,2,144,128]{4,3,2,1,0:T(8,128)}), f32[8,1,2,144,128]{4,3,2,1,0:T(8,128)}, u32[]{:S(2)}, u32[]{:S(2)}) async-start(f32[8,1,2,144,128]{4,3,2,1,0:T(8,128)} %bitcast.12), calls=%async_computation.2 | async-start | bytes 2359296 | tf_op jit(solution)/shard_map/all_to_all | solution.py:426
  150.7 17.8 %all-to-all-start.3 = ((f32[8,1,2,144,128]{4,3,2,1,0:T(8,128)}), f32[8,1,2,144,128]{4,3,2,1,0:T(8,128)S(1)}, u32[]{:S(2)}, u32[]{:S(2)}) async-start(f32[8,1,2,144,128]{4,3,2,1,0:T(8,128)} %bitcast.13), calls=%async_computation.3 | async-start | bytes 2359296 | tf_op jit(solution)/shard_map/all_to_all | solution.py:426
  (24 other events, 284.8 us)
